TPU v7x, 32 devices: a whole 2x2x4 slice. The times are simulated.
32 devices in a mesh: gy: 8 (over y, x, core), gz: 4 (over z).
Axes of the slice: x: 2, y: 2, z: 4, core: 2. Of those that a mesh axis runs over, the one named last changes fastest.
Arguments:
- efield_check: bfloat16 [3, 256, 8, 1024], P(None, 'gy', None, 'gz'), may hold values from -6 to 6
- hfield_check: bfloat16 [3, 256, 8, 1024], P(None, 'gy', None, 'gz'), may hold values from -6 to 6
- polar_check: bfloat16 [3, 256, 8, 1024], P(None, 'gy', None, 'gz'), may hold values from -4 to 4
- rate_check: bfloat16 [3, 256, 8, 1024], P(None, 'gy', None, 'gz'), may hold values from -4 to 4
- levels_check: bfloat16 [2, 256, 8, 1024], P(None, 'gy', None, 'gz'), may hold values from 0.049804688 to 0.5
- efield_seed: float32 [3, 256, 8, 1024], P(None, 'gy', None, 'gz'), may hold values from -6 to 6
- hfield_seed: float32 [3, 256, 8, 1024], P(None, 'gy', None, 'gz'), may hold values from -6 to 6
- polar_seed: float32 [3, 256, 8, 1024], P(None, 'gy', None, 'gz'), may hold values from -6 to 6
- rate_seed: float32 [3, 256, 8, 1024], P(None, 'gy', None, 'gz'), may hold values from -6 to 6
- levels_seed: float32 [2, 256, 8, 1024], P(None, 'gy', None, 'gz'), may hold values from -6 to 6
- material_labels: int32 [256, 8, 1024], P('gy', None, 'gz'), may hold values from 0 to 3
- gain_labels: int32 [256, 8, 1024], P('gy', None, 'gz'), may hold values 0 or 1
- inverse_table: float32 [4], replicated, may hold values from 0.08 to 1
- source_field: float32 [256, 8, 1024], P('gy', None, 'gz'), may hold values from -6 to 6
- start_step: int32 [1], replicated, may hold values from 0 to 255
Outputs:
- efield_grad: float32 [3, 256, 8, 1024], P(None, 'gy', None, 'gz')
- hfield_grad: float32 [3, 256, 8, 1024], P(None, 'gy', None, 'gz')
- polar_grad: float32 [3, 256, 8, 1024], P(None, 'gy', None, 'gz')
- rate_grad: float32 [3, 256, 8, 1024], P(None, 'gy', None, 'gz')
- levels_grad: float32 [2, 256, 8, 1024], P(None, 'gy', None, 'gz')
- cell_grad: float32 [256, 8, 1024], P('gy', None, 'gz')
- table_grad: float32 [4], replicated
All inputs are finite; a program needn't handle non-finite values. No bound on the sum of `gain_labels` on one device may be relied on, other than what follows from the above.
Results may differ from a plain program's by a relative error of at most 0.0003.
Values may be sent and summed in bfloat16 or wider, within the bound.
A program may use at most 64 MiB of HBM per device.

v0:
```python
import math

import jax
import jax.numpy as jnp
from jax import lax
from jax.sharding import PartitionSpec as P

MAGNETIC_STEP = 0.5
ELECTRIC_STEP = 0.5
TIME_STEP = 0.5
DAMPING = 0.9
STIFFNESS = 0.3
COUPLING = 0.4
PUMPING = 0.05
UPPER_DECAY = 0.02
LOWER_DECAY = 0.3
STIMULATED = 0.2
SOURCE_OMEGA = 0.35


def shifted(block, axis, distance):
    devices = range(lax.axis_size(axis))
    route = [(i - distance, i) for i in devices if i - distance in devices]
    return lax.ppermute(block, axis, route)


def front(values, axis):
    rest = lax.slice_in_dim(values, 1, values.shape[axis], axis=axis)
    border = jnp.zeros_like(lax.slice_in_dim(values, 0, 1, axis=axis))
    return jnp.concatenate([rest, border], axis)


def behind(values, axis):
    rest = lax.slice_in_dim(values, 0, values.shape[axis] - 1, axis=axis)
    border = jnp.zeros_like(lax.slice_in_dim(values, 0, 1, axis=axis))
    return jnp.concatenate([border, rest], axis)


def curl_from(along_x, along_y, along_z):
    return jnp.stack([along_y[2] - along_z[1], along_z[0] - along_x[2], along_x[1] - along_y[0]])


def curl_forward(field):
    front_row = shifted(field[:, :1], "gy", -1)
    front_column = shifted(field[:, :, :, :1], "gz", -1)
    along_y = jnp.concatenate([field[:, 1:], front_row], 1) - field
    along_z = jnp.concatenate([field[:, :, :, 1:], front_column], 3) - field
    along_x = front(field, 2) - field
    return curl_from(along_x, along_y, along_z)


def curl_backward(field):
    back_row = shifted(field[:, -1:], "gy", 1)
    back_column = shifted(field[:, :, :, -1:], "gz", 1)
    along_y = field - jnp.concatenate([back_row, field[:, :-1]], 1)
    along_z = field - jnp.concatenate([back_column, field[:, :, :, :-1]], 3)
    along_x = field - behind(field, 2)
    return curl_from(along_x, along_y, along_z)


def local_update(
    efield, polar_field, polar_rate, levels, curl_field, inverse, gain_region, source_push
):
    rate_next = (
        DAMPING * polar_rate
        - STIFFNESS * polar_field
        + COUPLING * gain_region * (levels[0] - levels[1]) * efield
    )
    polar_next = polar_field + TIME_STEP * rate_next
    forcing = ELECTRIC_STEP * curl_field - (polar_next - polar_field)
    forcing = jnp.concatenate([forcing[:2], forcing[2:] - source_push[None]], 0)
    efield_next = efield + inverse * forcing
    stimulated = STIMULATED * gain_region * jnp.sum(efield_next * rate_next, axis=0)
    upper = (
        levels[0]
        + TIME_STEP * (PUMPING * (1.0 - levels[0] - levels[1]) - UPPER_DECAY * levels[0])
        - stimulated
    )
    lower = levels[1] + TIME_STEP * (UPPER_DECAY * levels[0] - LOWER_DECAY * levels[1]) + stimulated
    return (efield_next, polar_next, rate_next, jnp.stack([upper, lower]))


def reverse_local(
    efield, polar_field, polar_rate, levels, curl_field, inverse, gain_region, source_push, seeds
):

    def update(first, second, third, fourth, fifth, sixth):
        return local_update(first, second, third, fourth, fifth, sixth, gain_region, source_push)

    unused, pullback = jax.vjp(update, efield, polar_field, polar_rate, levels, curl_field, inverse)
    return pullback(seeds)


def material_map(material_labels, inverse_table):
    inverse = jnp.zeros(material_labels.shape, jnp.float32)
    for label in range(inverse_table.shape[0]):
        inverse = inverse + jnp.where(
            material_labels == label, inverse_table[label], jnp.float32(0.0)
        )
    return inverse


def label_sums(material_labels, values, count):
    return jnp.stack(
        [
            jnp.sum(jnp.where(material_labels == label, values, jnp.float32(0.0)))
            for label in range(count)
        ]
    )


def on_device(
    efield_check,
    hfield_check,
    polar_check,
    rate_check,
    levels_check,
    efield_seed,
    hfield_seed,
    polar_seed,
    rate_seed,
    levels_seed,
    material_labels,
    gain_labels,
    inverse_table,
    source_field,
    start_step,
):
    count = inverse_table.shape[0]
    inverse = material_map(material_labels, inverse_table)
    gain_region = gain_labels.astype(jnp.float32)
    start = start_step[0].astype(jnp.float32)
    first_sine = jnp.sin(SOURCE_OMEGA * start)
    push_first = first_sine * source_field
    push_second = jnp.sin(SOURCE_OMEGA * (start + 1.0)) * source_field
    efield = efield_check.astype(jnp.float32)
    polar_field = polar_check.astype(jnp.float32)
    polar_rate = rate_check.astype(jnp.float32)
    levels = levels_check.astype(jnp.float32)
    hfield = hfield_check.astype(jnp.float32)
    hfield_mid = hfield - MAGNETIC_STEP * curl_forward(efield)
    curl_first = curl_backward(hfield_mid)
    state_one = local_update(
        efield, polar_field, polar_rate, levels, curl_first, inverse, gain_region, push_first
    )
    hfield_next = hfield_mid - MAGNETIC_STEP * curl_forward(state_one[0])
    curl_second = curl_backward(hfield_next)
    back_e, back_p, back_q, back_n, back_c, grad_second = reverse_local(
        state_one[0],
        state_one[1],
        state_one[2],
        state_one[3],
        curl_second,
        inverse,
        gain_region,
        push_second,
        (efield_seed, polar_seed, rate_seed, levels_seed),
    )
    h_back = hfield_seed + curl_forward(back_c)
    e_back = back_e - MAGNETIC_STEP * curl_backward(h_back)
    last_e, polar_grad, rate_grad, levels_grad, last_c, grad_first = reverse_local(
        efield,
        polar_field,
        polar_rate,
        levels,
        curl_first,
        inverse,
        gain_region,
        push_first,
        (e_back, back_p, back_q, back_n),
    )
    hfield_grad = h_back + curl_forward(last_c)
    efield_grad = last_e - MAGNETIC_STEP * curl_backward(hfield_grad)
    cell_grad = grad_second + grad_first
    cells = (
        material_labels.shape[0]
        * material_labels.shape[1]
        * material_labels.shape[2]
        * lax.axis_size("gy")
        * lax.axis_size("gz")
    )
    totals = lax.psum(label_sums(material_labels, cell_grad, count), ("gy", "gz"))
    table_grad = totals * (1.0 / math.sqrt(cells))
    return (efield_grad, hfield_grad, polar_grad, rate_grad, levels_grad, cell_grad, table_grad)


def solution(mesh):
    placed = (
        P(None, "gy", None, "gz"),
        P(None, "gy", None, "gz"),
        P(None, "gy", None, "gz"),
        P(None, "gy", None, "gz"),
        P(None, "gy", None, "gz"),
        P(None, "gy", None, "gz"),
        P(None, "gy", None, "gz"),
        P(None, "gy", None, "gz"),
        P(None, "gy", None, "gz"),
        P(None, "gy", None, "gz"),
        P("gy", None, "gz"),
        P("gy", None, "gz"),
        P(),
        P("gy", None, "gz"),
        P(),
    )
    return jax.shard_map(
        on_device,
        mesh=mesh,
        in_specs=placed,
        out_specs=(
            P(None, "gy", None, "gz"),
            P(None, "gy", None, "gz"),
            P(None, "gy", None, "gz"),
            P(None, "gy", None, "gz"),
            P(None, "gy", None, "gz"),
            P("gy", None, "gz"),
            P(),
        ),
        check_vma=False,
    )
```

profile of v0, /device:TPU:0, one launch (start us, length us, event | category | flops | bytes accessed | tf_op | source)
XLA Modules:
  0.0 152.7 jit_solution(13710361102462883744)
XLA Ops:
  1.7 1.3 collective-permute-start.1
  3.0 1.3 collective-permute-start
  6.2 9.5 %collective-permute-done.1 = f32[3,32,8,1]{3,2,1,0:T(8,128)S(1)} collective-permute-done((f32[3,32,8,1]{3,2,1,0:T(8,128)S(1)}, f32[3,32,8,1]{3,2,1,0:T(8,128)S(1)}, u32[]{:S(2)}, u32[]{:S(2)}) %collective-permute-start.1) | collective-permute-done | bytes 3104 | tf_op jit(solution)/shard_map/ppermute | solution.py:24
  17.3 3.7 %collective-permute-start.3 = (f32[3,32,8,1]{3,2,1,0:T(8,128)S(1)}, f32[3,32,8,1]{3,2,1,0:T(8,128)S(1)}, u32[]{:S(2)}, u32[]{:S(2)}) collective-permute-start(f32[3,32,8,1]{3,2,1,0:T(8,128)S(1)} %slice.423), channel_id=1, source_target_pairs={{0,1},{1,2},{2,3},{4,5},{5,6},{6,7},{8,9},{9,10},{10,11},{12,13},{... | collective-permute-start | bytes 9224 | tf_op jit(solution)/shard_map/ppermute | solution.py:24
  22.3 2.8 %select_add_fusion.2 = (f32[32,8,256]{2,1,0:T(8,128)S(1)}, pred[32,8,256]{2,1,0:T(8,128)(4,1)S(1)}, pred[32,8,256]{2,1,0:T(8,128)(4,1)S(1)}, pred[32,8,256]{2,1,...) fusion(f32[]{:T(128)} %bitcast.6, f32[]{:T(128)} %bitcast.5, f32[]{:T(128)} %bitcast.4, ...), kind=kLoop, calls=%fused_computation.114 | loop fusion | flops 983040 | bytes 1835024 | tf_op jit(solution)/shard_map/add | solution.py:97
  25.9 2.5 %collective-permute-done.3 = f32[3,32,8,1]{3,2,1,0:T(8,128)S(1)} collective-permute-done((f32[3,32,8,1]{3,2,1,0:T(8,128)S(1)}, f32[3,32,8,1]{3,2,1,0:T(8,128)S(1)}, u32[]{:S(2)}, u32[]{:S(2)}) %collective-permute-start.3) | collective-permute-done | bytes 3104 | tf_op jit(solution)/shard_map/ppermute | solution.py:24
  31.6 1.4 collective-permute-start.5
  33.1 1.3 collective-permute-start.4
  35.0 9.4 %collective-permute-done.5 = f32[3,32,8,1]{3,2,1,0:T(8,128)S(1)} collective-permute-done((f32[3,32,8,1]{3,2,1,0:T(8,128)S(1)}, f32[3,32,8,1]{3,2,1,0:T(8,128)S(1)}, u32[]{:S(2)}, u32[]{:S(2)}) %collective-permute-start.5) | collective-permute-done | bytes 3104 | tf_op jit(solution)/shard_map/ppermute | solution.py:24
  45.1 3.5 %collective-permute-start.7 = (f32[3,32,8,1]{3,2,1,0:T(8,128)S(1)}, f32[3,32,8,1]{3,2,1,0:T(8,128)S(1)}, u32[]{:S(2)}, u32[]{:S(2)}) collective-permute-start(f32[3,32,8,1]{3,2,1,0:T(8,128)S(1)} %slice.447), channel_id=1, source_target_pairs={{0,1},{1,2},{2,3},{4,5},{5,6},{6,7},{8,9},{9,10},{10,11},{12,13},{... | collective-permute-start | bytes 9224 | tf_op jit(solution)/shard_map/ppermute | solution.py:24
  50.2 4.8 %collective-permute-done.7 = f32[3,32,8,1]{3,2,1,0:T(8,128)S(1)} collective-permute-done((f32[3,32,8,1]{3,2,1,0:T(8,128)S(1)}, f32[3,32,8,1]{3,2,1,0:T(8,128)S(1)}, u32[]{:S(2)}, u32[]{:S(2)}) %collective-permute-start.7) | collective-permute-done | bytes 3104 | tf_op jit(solution)/shard_map/ppermute | solution.py:24
  59.6 1.3 collective-permute-start.9
  60.9 1.3 collective-permute-start.8
  63.6 6.9 %collective-permute-done.9 = f32[3,32,8,1]{3,2,1,0:T(8,128)S(1)} collective-permute-done((f32[3,32,8,1]{3,2,1,0:T(8,128)S(1)}, f32[3,32,8,1]{3,2,1,0:T(8,128)S(1)}, u32[]{:S(2)}, u32[]{:S(2)}) %collective-permute-start.9) | collective-permute-done | bytes 3104 | tf_op jit(solution)/shard_map/ppermute | solution.py:24
  72.5 3.3 %collective-permute-start.11 = (f32[3,32,8,1]{3,2,1,0:T(8,128)S(1)}, f32[3,32,8,1]{3,2,1,0:T(8,128)S(1)}, u32[]{:S(2)}, u32[]{:S(2)}) collective-permute-start(f32[3,32,8,1]{3,2,1,0:T(8,128)S(1)} %slice.471), channel_id=1, source_target_pairs={{0,1},{1,2},{2,3},{4,5},{5,6},{6,7},{8,9},{9,10},{10,11},{12,13},{... | collective-permute-start | bytes 9224 | tf_op jit(solution)/shard_map/ppermute | solution.py:24
  77.2 4.5 %collective-permute-done.11 = f32[3,32,8,1]{3,2,1,0:T(8,128)S(1)} collective-permute-done((f32[3,32,8,1]{3,2,1,0:T(8,128)S(1)}, f32[3,32,8,1]{3,2,1,0:T(8,128)S(1)}, u32[]{:S(2)}, u32[]{:S(2)}) %collective-permute-start.11) | collective-permute-done | bytes 3104 | tf_op jit(solution)/shard_map/ppermute | solution.py:24
  83.4 1.6 %multiply_add_fusion = (f32[3,32,8,256]{3,2,1,0:T(8,128)}, f32[3,32,8,256]{3,2,1,0:T(8,128)S(1)}, f32[3,32,8,256]{3,2,1,0:T(8,128)}) fusion(f32[3,32,8,256]{3,2,1,0:T(8,128)S(1)} %get-tuple-element.17, f32[3,32,8,256]{3,2,1,0:T(8,128)S(1)} %get-tuple-element.19, f32[3,32,8,256]{3,2,1,0:T(8,128)S(1)} %copy-done.6, pred[3]{0:T(512)(128)(4,1)S(1)} %copy-done.21, ...), kind=kLoop, calls=%fused_computation.46 | loop fusion | flops 3932160 | bytes 7077891 | tf_op jit(solution)/shard_map/transpose(jvp())/add_any | solution.py:66
  85.9 1.3 collective-permute-start.13
  87.2 1.3 collective-permute-start.12
  88.5 1.5 select_reduce_fusion.3
  90.0 2.6 %pad_maximum_fusion.2 = f32[4]{0:T(128)S(1)} fusion(f32[1]{0:T(128)} %bitcast.19, f32[1]{0:T(128)} %bitcast.18, f32[1]{0:T(128)} %bitcast.17, f32[1]{0:T(128)} %bitcast.16), kind=kLoop, calls=%fused_computation.128 | loop fusion | flops 12 | bytes 32 | tf_op jit(solution)/shard_map/stack | solution.py:104
  93.7 42.5 %psum.7 = f32[4]{0:T(128)S(1)} all-reduce(f32[4]{0:T(128)S(1)} %pad_maximum_fusion.2), channel_id=1, replica_groups=mesh['gy'=8,'gz'=4] {'gy','gz'}, use_global_device_ids=true, to_apply=%region_9.10 | all-reduce | flops 4 | bytes 32 | tf_op jit(solution)/shard_map/psum | solution.py:182
  139.5 4.1 %collective-permute-start.15 = (f32[3,32,8,1]{3,2,1,0:T(8,128)S(1)}, f32[3,32,8,1]{3,2,1,0:T(8,128)S(1)}, u32[]{:S(2)}, u32[]{:S(2)}) collective-permute-start(f32[3,32,8,1]{3,2,1,0:T(8,128)S(1)} %slice.493), channel_id=1, source_target_pairs={{0,1},{1,2},{2,3},{4,5},{5,6},{6,7},{8,9},{9,10},{10,11},{12,13},{... | collective-permute-start | bytes 9224 | tf_op jit(solution)/shard_map/ppermute | solution.py:24
  145.4 5.7 %collective-permute-done.15 = f32[3,32,8,1]{3,2,1,0:T(8,128)S(1)} collective-permute-done((f32[3,32,8,1]{3,2,1,0:T(8,128)S(1)}, f32[3,32,8,1]{3,2,1,0:T(8,128)S(1)}, u32[]{:S(2)}, u32[]{:S(2)}) %collective-permute-start.15) | collective-permute-done | bytes 3104 | tf_op jit(solution)/shard_map/ppermute | solution.py:24
  (138 shorter events, 31.1 us)
Async XLA Ops:
  0.6 2.3 %copy-start = (bf16[3,32,8,256]{3,2,1,0:T(8,128)(2,1)S(1)}, bf16[3,32,8,256]{3,2,1,0:T(8,128)(2,1)}, u32[]{:S(2)}) copy-start(bf16[3,32,8,256]{3,2,1,0:T(8,128)(2,1)} %param.15) | copy-start | bytes 1179652
  1.7 14.0 %collective-permute-start.1 = (f32[3,32,8,1]{3,2,1,0:T(8,128)S(1)}, f32[3,32,8,1]{3,2,1,0:T(8,128)S(1)}, u32[]{:S(2)}, u32[]{:S(2)}) collective-permute-start(f32[3,32,8,1]{3,2,1,0:T(8,128)S(1)} %slice.413), channel_id=1, source_target_pairs={{1,0},{2,1},{3,2},{5,4},{6,5},{7,6},{9,8},{10,9},{11,10},{13,12},{... | collective-permute-start | bytes 9224 | tf_op jit(solution)/shard_map/ppermute | solution.py:24
  3.0 12.7 %collective-permute-start = (f32[3,1,8,256]{3,2,1,0:T(8,128)S(1)}, f32[3,1,8,256]{3,2,1,0:T(8,128)S(1)}, u32[]{:S(2)}, u32[]{:S(2)}) collective-permute-start(f32[3,1,8,256]{3,2,1,0:T(8,128)S(1)} %slice.410), channel_id=1, source_target_pairs={{4,0},{8,4},{12,8},{16,12},{20,16},{24,20},{28,24},{5,1},{9,5},{13... | collective-permute-start | bytes 73736 | tf_op jit(solution)/shard_map/ppermute | solution.py:24
  17.1 5.2 %copy-start.13 = (s32[32,8,256]{2,1,0:T(8,128)S(1)}, s32[32,8,256]{2,1,0:T(8,128)}, u32[]{:S(2)}) copy-start(s32[32,8,256]{2,1,0:T(8,128)} %param.26) | copy-start | bytes 786436
  17.1 5.2 %copy-start.19 = (s32[32,8,256]{2,1,0:T(8,128)S(1)}, s32[32,8,256]{2,1,0:T(8,128)}, u32[]{:S(2)}) copy-start(s32[32,8,256]{2,1,0:T(8,128)} %param.25) | copy-start | bytes 786436
  17.3 11.1 %collective-permute-start.3 = (f32[3,32,8,1]{3,2,1,0:T(8,128)S(1)}, f32[3,32,8,1]{3,2,1,0:T(8,128)S(1)}, u32[]{:S(2)}, u32[]{:S(2)}) collective-permute-start(f32[3,32,8,1]{3,2,1,0:T(8,128)S(1)} %slice.423), channel_id=1, source_target_pairs={{0,1},{1,2},{2,3},{4,5},{5,6},{6,7},{8,9},{9,10},{10,11},{12,13},{... | collective-permute-start | bytes 9224 | tf_op jit(solution)/shard_map/ppermute | solution.py:24
  20.9 7.5 %collective-permute-start.2 = (f32[3,1,8,256]{3,2,1,0:T(8,128)S(1)}, f32[3,1,8,256]{3,2,1,0:T(8,128)S(1)}, u32[]{:S(2)}, u32[]{:S(2)}) collective-permute-start(f32[3,1,8,256]{3,2,1,0:T(8,128)S(1)} %slice.420), channel_id=1, source_target_pairs={{0,4},{4,8},{8,12},{12,16},{16,20},{20,24},{24,28},{1,5},{5,9},{9,... | collective-permute-start | bytes 73736 | tf_op jit(solution)/shard_map/ppermute | solution.py:24
  31.6 2.8 %copy-start.5 = (f32[2,32,8,256]{3,2,1,0:T(8,128)S(1)}, f32[2,32,8,256]{3,2,1,0:T(8,128)}, u32[]{:S(2)}) copy-start(f32[2,32,8,256]{3,2,1,0:T(8,128)} %param.24) | copy-start | bytes 1572868
  31.6 12.8 %collective-permute-start.5 = (f32[3,32,8,1]{3,2,1,0:T(8,128)S(1)}, f32[3,32,8,1]{3,2,1,0:T(8,128)S(1)}, u32[]{:S(2)}, u32[]{:S(2)}) collective-permute-start(f32[3,32,8,1]{3,2,1,0:T(8,128)S(1)} %slice.437), channel_id=1, source_target_pairs={{1,0},{2,1},{3,2},{5,4},{6,5},{7,6},{9,8},{10,9},{11,10},{13,12},{... | collective-permute-start | bytes 9224 | tf_op jit(solution)/shard_map/ppermute | solution.py:24
  33.1 11.3 %collective-permute-start.4 = (f32[3,1,8,256]{3,2,1,0:T(8,128)S(1)}, f32[3,1,8,256]{3,2,1,0:T(8,128)S(1)}, u32[]{:S(2)}, u32[]{:S(2)}) collective-permute-start(f32[3,1,8,256]{3,2,1,0:T(8,128)S(1)} %slice.434), channel_id=1, source_target_pairs={{4,0},{8,4},{12,8},{16,12},{20,16},{24,20},{28,24},{5,1},{9,5},{13... | collective-permute-start | bytes 73736 | tf_op jit(solution)/shard_map/ppermute | solution.py:24
  45.1 9.9 %collective-permute-start.7 = (f32[3,32,8,1]{3,2,1,0:T(8,128)S(1)}, f32[3,32,8,1]{3,2,1,0:T(8,128)S(1)}, u32[]{:S(2)}, u32[]{:S(2)}) collective-permute-start(f32[3,32,8,1]{3,2,1,0:T(8,128)S(1)} %slice.447), channel_id=1, source_target_pairs={{0,1},{1,2},{2,3},{4,5},{5,6},{6,7},{8,9},{9,10},{10,11},{12,13},{... | collective-permute-start | bytes 9224 | tf_op jit(solution)/shard_map/ppermute | solution.py:24
  48.6 6.4 %collective-permute-start.6 = (f32[3,1,8,256]{3,2,1,0:T(8,128)S(1)}, f32[3,1,8,256]{3,2,1,0:T(8,128)S(1)}, u32[]{:S(2)}, u32[]{:S(2)}) collective-permute-start(f32[3,1,8,256]{3,2,1,0:T(8,128)S(1)} %slice.444), channel_id=1, source_target_pairs={{0,4},{4,8},{8,12},{12,16},{16,20},{20,24},{24,28},{1,5},{5,9},{9,... | collective-permute-start | bytes 73736 | tf_op jit(solution)/shard_map/ppermute | solution.py:24
  59.6 11.0 %collective-permute-start.9 = (f32[3,32,8,1]{3,2,1,0:T(8,128)S(1)}, f32[3,32,8,1]{3,2,1,0:T(8,128)S(1)}, u32[]{:S(2)}, u32[]{:S(2)}) collective-permute-start(f32[3,32,8,1]{3,2,1,0:T(8,128)S(1)} %slice.461), channel_id=1, source_target_pairs={{1,0},{2,1},{3,2},{5,4},{6,5},{7,6},{9,8},{10,9},{11,10},{13,12},{... | collective-permute-start | bytes 9224 | tf_op jit(solution)/shard_map/ppermute | solution.py:24
  60.9 9.7 %collective-permute-start.8 = (f32[3,1,8,256]{3,2,1,0:T(8,128)S(1)}, f32[3,1,8,256]{3,2,1,0:T(8,128)S(1)}, u32[]{:S(2)}, u32[]{:S(2)}) collective-permute-start(f32[3,1,8,256]{3,2,1,0:T(8,128)S(1)} %slice.458), channel_id=1, source_target_pairs={{4,0},{8,4},{12,8},{16,12},{20,16},{24,20},{28,24},{5,1},{9,5},{13... | collective-permute-start | bytes 73736 | tf_op jit(solution)/shard_map/ppermute | solution.py:24
  71.1 10.6 %copy-start.7 = (f32[1,32,8,256]{3,2,1,0:T(8,128)}, f32[1,32,8,256]{3,2,1,0:T(8,128)S(1)}, u32[]{:S(2)}) copy-start(f32[1,32,8,256]{3,2,1,0:T(8,128)S(1)} %get-tuple-element.52) | copy-start | bytes 786436
  71.1 10.6 %copy-start.9 = (f32[1,32,8,256]{3,2,1,0:T(8,128)}, f32[1,32,8,256]{3,2,1,0:T(8,128)S(1)}, u32[]{:S(2)}) copy-start(f32[1,32,8,256]{3,2,1,0:T(8,128)S(1)} %get-tuple-element.53) | copy-start | bytes 786436
  71.1 10.6 %copy-start.11 = (f32[1,32,8,256]{3,2,1,0:T(8,128)}, f32[1,32,8,256]{3,2,1,0:T(8,128)S(1)}, u32[]{:S(2)}) copy-start(f32[1,32,8,256]{3,2,1,0:T(8,128)S(1)} %get-tuple-element.54) | copy-start | bytes 786436
  72.5 9.2 %collective-permute-start.11 = (f32[3,32,8,1]{3,2,1,0:T(8,128)S(1)}, f32[3,32,8,1]{3,2,1,0:T(8,128)S(1)}, u32[]{:S(2)}, u32[]{:S(2)}) collective-permute-start(f32[3,32,8,1]{3,2,1,0:T(8,128)S(1)} %slice.471), channel_id=1, source_target_pairs={{0,1},{1,2},{2,3},{4,5},{5,6},{6,7},{8,9},{9,10},{10,11},{12,13},{... | collective-permute-start | bytes 9224 | tf_op jit(solution)/shard_map/ppermute | solution.py:24
  75.8 5.9 %collective-permute-start.10 = (f32[3,1,8,256]{3,2,1,0:T(8,128)S(1)}, f32[3,1,8,256]{3,2,1,0:T(8,128)S(1)}, u32[]{:S(2)}, u32[]{:S(2)}) collective-permute-start(f32[3,1,8,256]{3,2,1,0:T(8,128)S(1)} %slice.468), channel_id=1, source_target_pairs={{0,4},{4,8},{8,12},{12,16},{16,20},{20,24},{24,28},{1,5},{5,9},{9,... | collective-permute-start | bytes 73736 | tf_op jit(solution)/shard_map/ppermute | solution.py:24
  85.9 50.8 %collective-permute-start.13 = (f32[3,32,8,1]{3,2,1,0:T(8,128)}, f32[3,32,8,1]{3,2,1,0:T(8,128)}, u32[]{:S(2)}, u32[]{:S(2)}) collective-permute-start(f32[3,32,8,1]{3,2,1,0:T(8,128)} %slice.483), channel_id=1, source_target_pairs={{1,0},{2,1},{3,2},{5,4},{6,5},{7,6},{9,8},{10,9},{11,10},{13,12},{... | collective-permute-start | bytes 9224 | tf_op jit(solution)/shard_map/ppermute | solution.py:24
  87.2 49.5 %collective-permute-start.12 = (f32[3,1,8,256]{3,2,1,0:T(8,128)S(1)}, f32[3,1,8,256]{3,2,1,0:T(8,128)S(1)}, u32[]{:S(2)}, u32[]{:S(2)}) collective-permute-start(f32[3,1,8,256]{3,2,1,0:T(8,128)S(1)} %slice.480), channel_id=1, source_target_pairs={{4,0},{8,4},{12,8},{16,12},{20,16},{24,20},{28,24},{5,1},{9,5},{13... | collective-permute-start | bytes 73736 | tf_op jit(solution)/shard_map/ppermute | solution.py:24
  139.3 11.8 %copy-start.1 = (f32[3,32,8,256]{3,2,1,0:T(8,128)}, f32[3,32,8,256]{3,2,1,0:T(8,128)S(1)}, u32[]{:S(2)}) copy-start(f32[3,32,8,256]{3,2,1,0:T(8,128)S(1)} %maximum_add_fusion.1) | copy-start | bytes 2359300
  139.5 11.6 %collective-permute-start.15 = (f32[3,32,8,1]{3,2,1,0:T(8,128)S(1)}, f32[3,32,8,1]{3,2,1,0:T(8,128)S(1)}, u32[]{:S(2)}, u32[]{:S(2)}) collective-permute-start(f32[3,32,8,1]{3,2,1,0:T(8,128)S(1)} %slice.493), channel_id=1, source_target_pairs={{0,1},{1,2},{2,3},{4,5},{5,6},{6,7},{8,9},{9,10},{10,11},{12,13},{... | collective-permute-start | bytes 9224 | tf_op jit(solution)/shard_map/ppermute | solution.py:24
  143.5 7.5 %collective-permute-start.14 = (f32[3,1,8,256]{3,2,1,0:T(8,128)S(1)}, f32[3,1,8,256]{3,2,1,0:T(8,128)S(1)}, u32[]{:S(2)}, u32[]{:S(2)}) collective-permute-start(f32[3,1,8,256]{3,2,1,0:T(8,128)S(1)} %slice.490), channel_id=1, source_target_pairs={{0,4},{4,8},{8,12},{12,16},{16,20},{20,24},{24,28},{1,5},{5,9},{9,... | collective-permute-start | bytes 73736 | tf_op jit(solution)/shard_map/ppermute | solution.py:24
  (15 other events, 16.3 us)
where the time goes:
time: 154 us; the launch traced here: 153 us
  waiting for transfers between devices  43.3 us (28%)
  blocking collectives  42.5 us (28%)
  starting transfers between devices  30.1 us (20%)
  other arithmetic  20.8 us (14%)
  local copies, waits for them, and re-layouts  13.7 us (9%)
  between operations  2.25 us (1%)
    ppermute x16, waiting for transfers between devices, shifted(): return lax.ppermute(block, axis, route)  43.3 us
    psum x1, blocking collectives, on_device(): lax.psum(label_sums(material_labels, cell_grad, count), ('gy', 'gz'))  42.5 us
    ppermute x16, starting transfers between devices, shifted(): return lax.ppermute(block, axis, route)  30.1 us
    unnamed x46, local copies, waits for them, and re-layouts  8.78 us
  transfers between devices with their start and end apart: 16, of which 7 were waited for; matrix products, arithmetic and copies ran while one was open for 8% of the time, Pallas kernels for 0%

commit v1 on v0

v1 whole, which is shorter than its diff:
```python
import functools
import math

import jax
import jax.numpy as jnp
from jax import lax
from jax.experimental import pallas as pl
from jax.experimental.pallas import tpu as pltpu
from jax.sharding import PartitionSpec as P

MAGNETIC_STEP = 0.5
ELECTRIC_STEP = 0.5
TIME_STEP = 0.5
DAMPING = 0.9
STIFFNESS = 0.3
COUPLING = 0.4
PUMPING = 0.05
UPPER_DECAY = 0.02
LOWER_DECAY = 0.3
STIMULATED = 0.2
SOURCE_OMEGA = 0.35

MESH = pl.DeviceIdType.MESH
LANES = 128
FIELDS = (1, 2, 1)
BASES = (2, 2, 0)
UP = tuple(3 * f + b for f, b in zip(FIELDS, BASES))
DOWN = tuple(2 * f for f in FIELDS)
UP_AT = tuple(sum(UP[:k]) for k in range(3))
DOWN_AT = tuple(sum(DOWN[:k]) for k in range(3))
DIAG_AT = tuple(sum(FIELDS[:k]) for k in range(3))


def kernel(
    ngy,
    ngz,
    count,
    scale,
    e_in, h_in, p_in, q_in, n_in,
    es_in, hs_in, ps_in, qs_in, ns_in,
    lab_in, gain_in, table, src_in, start,
    eg_out, hg_out, pg_out, qg_out, ng_out, cg_out, tg_out,
    e_v, h_v, p_v, q_v, n_v,
    es_v, hs_v, ps_v, qs_v, ns_v,
    lab_v, gain_v, src_v,
    ef, m, e1, ac, q1, q2, f1, k1, cc, hg, eg, pg, qg, ng, cg,
    m_col, b_col,
    yu_s, yu_r, yd_s, yd_r, zu_s, zu_r, zd_s, zd_r, a_r, b_r,
    sums, part_z, part_y,
    in_sem, out_sem, send_sem, recv_sem,
    zs_sem, zr_sem, ys_sem, yr_sem,
):
    gy = lax.axis_index("gy")
    gz = lax.axis_index("gz")
    rows, depth, width = e_v.shape[1], e_v.shape[2], e_v.shape[3]

    pairs = (
        (e_in, e_v), (h_in, h_v), (q_in, q_v), (p_in, p_v), (n_in, n_v),
        (lab_in, lab_v), (gain_in, gain_v), (src_in, src_v), (es_in, es_v),
        (ns_in, ns_v), (hs_in, hs_v), (qs_in, qs_v), (ps_in, ps_v),
    )
    loads = [
        pltpu.make_async_copy(a, b, in_sem.at[i]) for i, (a, b) in enumerate(pairs)
    ]
    for copy in loads:
        copy.start()

    for ref in (yu_r, yd_r, zu_r, zd_r, a_r, b_r, zu_s, zd_s):
        ref[...] = jnp.zeros(ref.shape, ref.dtype)

    has_down, has_up = gy > 0, gy < ngy - 1
    has_left, has_right = gz > 0, gz < ngz - 1
    diag_a = jnp.logical_and(has_up, has_left)
    diag_b = jnp.logical_and(has_down, has_right)

    barrier = pltpu.get_barrier_semaphore()

    def greet_y(d, _):
        pl.semaphore_signal(
            barrier, inc=1, device_id=(lax.rem(gy + d, ngy), gz), device_id_type=MESH
        )
        return _

    def greet_z(d, _):
        pl.semaphore_signal(
            barrier, inc=1, device_id=(gy, lax.rem(gz + d, ngz)), device_id_type=MESH
        )
        return _

    lax.fori_loop(1, ngy, greet_y, 0)
    lax.fori_loop(1, ngz, greet_z, 0)

    @pl.when(diag_a)
    def _():
        pl.semaphore_signal(barrier, inc=1, device_id=(gy + 1, gz - 1), device_id_type=MESH)

    @pl.when(diag_b)
    def _():
        pl.semaphore_signal(barrier, inc=1, device_id=(gy - 1, gz + 1), device_id_type=MESH)

    def links(k):
        f = FIELDS[k]
        up = pl.ds(UP_AT[k], UP[k])
        down = pl.ds(DOWN_AT[k], DOWN[k])
        diag = pl.ds(DIAG_AT[k], f)
        return (
            (yu_s.at[up], yu_r.at[up], (gy + 1, gz), has_up, has_down),
            (yd_s.at[down], yd_r.at[down], (gy - 1, gz), has_down, has_up),
            (zu_s.at[up], zu_r.at[up], (gy, gz + 1), has_right, has_left),
            (zd_s.at[down], zd_r.at[down], (gy, gz - 1), has_left, has_right),
            (zd_s.at[pl.ds(DOWN_AT[k] + f, f)], a_r.at[diag], (gy + 1, gz - 1), diag_a, diag_b),
            (zu_s.at[pl.ds(UP_AT[k] + 2 * f, f)], b_r.at[diag], (gy - 1, gz + 1), diag_b, diag_a),
        )

    def remote(k, i, link):
        return pltpu.make_async_remote_copy(
            src_ref=link[0],
            dst_ref=link[1],
            send_sem=send_sem.at[k, i],
            recv_sem=recv_sem.at[k, i],
            device_id=link[2],
            device_id_type=MESH,
        )

    def send(k):
        for i, link in enumerate(links(k)):

            @pl.when(link[3])
            def _(i=i, link=link):
                remote(k, i, link).start()

    def receive(k):
        for i, link in enumerate(links(k)):

            @pl.when(link[4])
            def _(i=i, link=link):
                remote(k, i, link).wait_recv()

    def finish(k):
        for i, link in enumerate(links(k)):

            @pl.when(link[3])
            def _(i=i, link=link):
                remote(k, i, link).wait_send()

    lane_wide = lax.broadcasted_iota(jnp.int32, (depth, width), 1)
    sub_wide = lax.broadcasted_iota(jnp.int32, (depth, width), 0)
    lane = lax.broadcasted_iota(jnp.int32, (depth, LANES), 1)
    sub = lax.broadcasted_iota(jnp.int32, (depth, LANES), 0)
    last_lane = lane_wide == width - 1
    first_lane = lane_wide == 0
    tiles = width // LANES

    def widen(tile):
        return tile if tiles == 1 else jnp.concatenate([tile] * tiles, axis=1)

    def x_front(v):
        s = sub_wide if v.shape[1] == width else sub
        return jnp.where(s == depth - 1, 0.0, pltpu.roll(v, depth - 1, 0))

    def x_behind(v):
        return jnp.where(sub_wide == 0, 0.0, pltpu.roll(v, 1, 0))

    def z_front(v, tile, r):
        border = pltpu.roll(tile, LANES - 1 - r, 1)
        return jnp.where(last_lane, widen(border), pltpu.roll(v, width - 1, 1))

    def z_behind(v, tile, r):
        border = pltpu.roll(tile, lax.rem(LANES - r, LANES), 1)
        return jnp.where(first_lane, widen(border), pltpu.roll(v, 1, 1))

    def curl_forward(ref, k, j, r):
        f = FIELDS[k]
        vx, vy, vz = ref[0, r], ref[1, r], ref[2, r]
        dy_x, dy_z = ref[0, r + 1] - vx, ref[2, r + 1] - vz
        dz_x = z_front(vx, zd_r[DOWN_AT[k] + j], r) - vx
        dz_y = z_front(vy, zd_r[DOWN_AT[k] + f + j], r) - vy
        dx_y, dx_z = x_front(vy) - vy, x_front(vz) - vz
        return (dy_z - dz_y, dz_x - dx_z, dx_y - dy_x)

    def curl_backward(vx, vy, vz, back_x, back_z, col, r):
        dy_x, dy_z = vx - back_x, vz - back_z
        dz_x = vx - z_behind(vx, col[0], r)
        dz_y = vy - z_behind(vy, col[1], r)
        dx_y, dx_z = vy - x_behind(vy), vz - x_behind(vz)
        return (dy_z - dz_y, dz_x - dx_z, dx_y - dy_x)

    def border_row(ref, k, j):
        f = FIELDS[k]
        vx, vy, vz = (yu_r[UP_AT[k] + c * f + j] for c in range(3))
        dz_y = z_front(vy, a_r[DIAG_AT[k] + j], rows - 1) - vy
        dy_x, dy_z = ref[0, 0] - vx, ref[2, 0] - vz
        return dy_z - dz_y, x_front(vy) - vy - dy_x

    def border_col(k, j):
        f = FIELDS[k]
        vx, vy, vz = (zu_r[UP_AT[k] + c * f + j] for c in range(3))
        corner = pltpu.roll(b_r[DIAG_AT[k] + j], rows - 1, 1)
        dy_z = jnp.where(lane == rows - 1, corner, pltpu.roll(vz, LANES - 1, 1)) - vz
        dz_x = zd_s[DOWN_AT[k] + j] - vx
        dz_y = zd_s[DOWN_AT[k] + f + j] - vy
        return dy_z - dz_y, dz_x - (x_front(vz) - vz)

    row_on = jnp.where(has_down, 1.0, 0.0).astype(jnp.float32)
    col_on = jnp.where(has_left, 1.0, 0.0).astype(jnp.float32)

    def pack(ref, slot, r, column):
        ref[slot] = jnp.where(lane == r, jnp.broadcast_to(column, (depth, LANES)), ref[slot])

    def pack_first(k, j, r, vx, vy):
        f = FIELDS[k]
        pack(zd_s, DOWN_AT[k] + j, r, vx[:, :1])
        pack(zd_s, DOWN_AT[k] + f + j, r, vy[:, :1])

    def pack_last(k, j, r, values):
        f = FIELDS[k]
        for c, v in enumerate(values):
            pack(zu_s, UP_AT[k] + c * f + j, r, v[:, width - 1 :])

    def pack_base(k, r, vx, vy):
        pack(zu_s, UP_AT[k] + 3 * FIELDS[k], r, vx[:, width - 1 :])
        pack(zu_s, UP_AT[k] + 3 * FIELDS[k] + 1, r, vy[:, width - 1 :])

    def stage_rows(k, j, ref):
        f = FIELDS[k]
        for c in range(3):
            yu_s[UP_AT[k] + c * f + j] = ref[c, rows - 1]
        yd_s[DOWN_AT[k] + j] = ref[0, 0]
        yd_s[DOWN_AT[k] + f + j] = ref[2, 0]

    def take_rows(k, j, ref):
        f = FIELDS[k]
        ref[0, rows] = yd_r[DOWN_AT[k] + j]
        ref[2, rows] = yd_r[DOWN_AT[k] + f + j]

    loads[0].wait()
    loads[1].wait()

    def first_pass(r, _):
        v = [e_v[c, r].astype(jnp.float32) for c in range(3)]
        for c in range(3):
            ef[c, r] = v[c]
        pack_first(0, 0, r, v[0], v[1])
        pack_last(0, 0, r, v)
        pack_base(0, r, h_v[0, r].astype(jnp.float32), h_v[1, r].astype(jnp.float32))
        return _

    lax.fori_loop(0, rows, first_pass, 0)
    stage_rows(0, 0, ef)
    yu_s[UP_AT[0] + 3] = h_v[0, rows - 1].astype(jnp.float32)
    yu_s[UP_AT[0] + 4] = h_v[2, rows - 1].astype(jnp.float32)

    greeted = (
        (ngy - 1) + (ngz - 1) + jnp.where(diag_a, 1, 0) + jnp.where(diag_b, 1, 0)
    )
    pl.semaphore_wait(barrier, greeted)
    send(0)

    begin = start[0].astype(jnp.float32)
    sine_first = jnp.sin(jnp.full((depth, LANES), SOURCE_OMEGA * begin, jnp.float32))
    sine_second = jnp.sin(jnp.full((depth, LANES), SOURCE_OMEGA * (begin + 1.0), jnp.float32))
    sine_first, sine_second = widen(sine_first), widen(sine_second)

    for copy in loads[2:11]:
        copy.wait()

    def inverse_of(labels):
        value = jnp.full(labels.shape, table[0], jnp.float32)
        for label in range(1, count):
            value = jnp.where(labels == label, table[label], value)
        return value

    receive(0)
    take_rows(0, 0, ef)
    row_x, row_z = border_row(ef, 0, 0)
    m[0, 0] = row_on * (yu_r[UP_AT[0] + 3] - MAGNETIC_STEP * row_x)
    m[2, 0] = row_on * (yu_r[UP_AT[0] + 4] - MAGNETIC_STEP * row_z)
    col_x, col_y = border_col(0, 0)
    m_col[0] = col_on * (zu_r[UP_AT[0] + 3] - MAGNETIC_STEP * col_x)
    m_col[1] = col_on * (zu_r[UP_AT[0] + 4] - MAGNETIC_STEP * col_y)

    def forward_pass(r, _):
        curl = curl_forward(ef, 0, 0, r)
        mid = [h_v[c, r].astype(jnp.float32) - MAGNETIC_STEP * curl[c] for c in range(3)]
        for c in range(3):
            m[c, r + 1] = mid[c]
        c1 = curl_backward(*mid, m[0, r], m[2, r], m_col, r)
        inverse = inverse_of(lab_v[r])
        gain = gain_v[r].astype(jnp.float32)
        source = src_v[r]
        upper, lower = n_v[0, r].astype(jnp.float32), n_v[1, r].astype(jnp.float32)
        gain_c, gain_s = COUPLING * gain, STIMULATED * gain
        couple = gain_c * (upper - lower)
        nexts, rates, polars = [], [], []
        work = None
        for c in range(3):
            e, p, q = ef[c, r], p_v[c, r].astype(jnp.float32), q_v[c, r].astype(jnp.float32)
            rate = DAMPING * q - STIFFNESS * p + couple * e
            polars.append(p + TIME_STEP * rate)
            force = ELECTRIC_STEP * c1[c] - TIME_STEP * rate
            if c == 2:
                force = force - sine_first * source
            new = e + inverse * force
            q1[c, r] = rate
            f1[c, r] = force
            e1[c, r] = new
            work = new * rate if work is None else work + new * rate
            nexts.append(new)
            rates.append(rate)
        s = gain_s * work
        upper_1 = upper + TIME_STEP * (PUMPING * (1.0 - upper - lower) - UPPER_DECAY * upper) - s
        lower_1 = lower + TIME_STEP * (UPPER_DECAY * upper - LOWER_DECAY * lower) + s
        couple_1 = gain_c * (upper_1 - lower_1)
        k1[r] = couple_1
        t2 = gain_s * (ns_v[1, r] - ns_v[0, r])
        half = ELECTRIC_STEP * inverse
        adj = []
        for c in range(3):
            rate = DAMPING * rates[c] - STIFFNESS * polars[c] + couple_1 * nexts[c]
            q2[c, r] = rate
            adj.append(half * (es_v[c, r] + t2 * rate))
            ac[c, r] = adj[c]
        pack_first(1, 0, r, nexts[0], nexts[1])
        pack_last(1, 0, r, nexts)
        pack_first(1, 1, r, adj[0], adj[1])
        pack_last(1, 1, r, adj)
        pack_base(1, r, hs_v[0, r], hs_v[1, r])
        return _

    lax.fori_loop(0, rows, forward_pass, 0)

    stage_rows(1, 0, e1)
    stage_rows(1, 1, ac)
    yu_s[UP_AT[1] + 6] = hs_v[0, rows - 1]
    yu_s[UP_AT[1] + 7] = hs_v[2, rows - 1]
    send(1)
    for copy in loads[11:]:
        copy.wait()
    receive(1)
    take_rows(1, 0, e1)
    take_rows(1, 1, ac)
    row_x, row_z = border_row(e1, 1, 0)
    m[0, 0] = m[0, 0] - MAGNETIC_STEP * (row_on * row_x)
    m[2, 0] = m[2, 0] - MAGNETIC_STEP * (row_on * row_z)
    row_x, row_z = border_row(ac, 1, 1)
    hg[0, 0] = row_on * (yu_r[UP_AT[1] + 6] + row_x)
    hg[2, 0] = row_on * (yu_r[UP_AT[1] + 7] + row_z)
    col_x, col_y = border_col(1, 0)
    m_col[0] = m_col[0] - MAGNETIC_STEP * (col_on * col_x)
    m_col[1] = m_col[1] - MAGNETIC_STEP * (col_on * col_y)
    col_x, col_y = border_col(1, 1)
    b_col[0] = col_on * (zu_r[UP_AT[1] + 6] + col_x)
    b_col[1] = col_on * (zu_r[UP_AT[1] + 7] + col_y)
    sums[...] = jnp.zeros(sums.shape, jnp.float32)

    keep_upper = 1.0 - TIME_STEP * (PUMPING + UPPER_DECAY)
    feed_upper = TIME_STEP * UPPER_DECAY
    drain_lower = -TIME_STEP * PUMPING
    keep_lower = 1.0 - TIME_STEP * LOWER_DECAY

    def backward_pass(r, _):
        curl = curl_forward(e1, 1, 0, r)
        last = [m[c, r + 1] - MAGNETIC_STEP * curl[c] for c in range(3)]
        back_x, back_z = m[0, r], m[2, r]
        m[0, r + 1] = last[0]
        m[2, r + 1] = last[2]
        c2 = curl_backward(*last, back_x, back_z, m_col, r)
        curl = curl_forward(ac, 1, 1, r)
        hb = [hs_v[c, r] + curl[c] for c in range(3)]
        for c in range(3):
            hg[c, r + 1] = hb[c]
        eb = curl_backward(*hb, hg[0, r], hg[2, r], b_col, r)

        labels = lab_v[r]
        inverse = inverse_of(labels)
        gain = gain_v[r].astype(jnp.float32)
        source = src_v[r]
        gain_c, gain_s = COUPLING * gain, STIMULATED * gain
        seed_u, seed_l = ns_v[0, r], ns_v[1, r]
        t2 = gain_s * (seed_l - seed_u)
        couple_1 = k1[r]
        total = None
        overlap = None
        b_e, a_p, a_q = [], [], []
        for c in range(3):
            e, rate = e1[c, r], q2[c, r]
            force = ELECTRIC_STEP * c2[c] - TIME_STEP * rate
            if c == 2:
                force = force - sine_second * source
            new = e + inverse * force
            adj_e = es_v[c, r] + t2 * rate
            term = adj_e * force
            total = term if total is None else total + term
            seed_p = ps_v[c, r]
            adj_q = qs_v[c, r] + t2 * new + TIME_STEP * (seed_p - inverse * adj_e)
            a_p.append(seed_p - STIFFNESS * adj_q)
            a_q.append(DAMPING * adj_q)
            b_e.append(adj_e + couple_1 * adj_q - MAGNETIC_STEP * eb[c])
            overlap = adj_q * e if overlap is None else overlap + adj_q * e
        bend = gain_c * overlap
        a_u = keep_upper * seed_u + feed_upper * seed_l + bend
        a_l = drain_lower * seed_u + keep_lower * seed_l - bend

        t1 = gain_s * (a_l - a_u)
        upper, lower = n_v[0, r].astype(jnp.float32), n_v[1, r].astype(jnp.float32)
        couple = gain_c * (upper - lower)
        overlap = None
        out = []
        for c in range(3):
            rate = q1[c, r]
            adj_e = b_e[c] + t1 * rate
            total = total + adj_e * f1[c, r]
            adj_f = inverse * adj_e
            curl_adj = ELECTRIC_STEP * adj_f
            out.append(curl_adj)
            cc[c, r] = curl_adj
            adj_q = a_q[c] + t1 * e1[c, r] + TIME_STEP * (a_p[c] - adj_f)
            pg[c, r] = a_p[c] - STIFFNESS * adj_q
            qg[c, r] = DAMPING * adj_q
            eg[c, r] = adj_e + couple * adj_q
            e = ef[c, r]
            overlap = adj_q * e if overlap is None else overlap + adj_q * e
        bend = gain_c * overlap
        ng[0, r] = keep_upper * a_u + feed_upper * a_l + bend
        ng[1, r] = drain_lower * a_u + keep_lower * a_l - bend
        cg[r] = total
        for label in range(count):
            sums[label] = sums[label] + jnp.where(labels == label, total, 0.0)
        pack_first(2, 0, r, out[0], out[1])
        pack_last(2, 0, r, out)
        return _

    lax.fori_loop(0, rows, backward_pass, 0)

    stage_rows(2, 0, cc)
    send(2)

    stores = [
        pltpu.make_async_copy(a, b, out_sem.at[i])
        for i, (a, b) in enumerate(
            (
                (pg, pg_out), (qg, qg_out), (ng, ng_out), (cg, cg_out),
                (hg.at[:, pl.ds(1, rows)], hg_out), (eg, eg_out),
            )
        )
    ]
    for copy in stores[:4]:
        copy.start()

    mine = jnp.zeros(part_z.shape[1:], jnp.float32)
    part_sub = lax.broadcasted_iota(jnp.int32, mine.shape, 0)
    for label in range(count):
        narrow = sum(sums[label, :, t * LANES : (t + 1) * LANES] for t in range(tiles))
        mine = jnp.where(part_sub == label, jnp.sum(narrow, axis=0, keepdims=True), mine)
    part_z[gz] = mine

    def gather(part, n, me, device, s_sem, r_sem):
        def copy_to(d):
            return pltpu.make_async_remote_copy(
                src_ref=part.at[me],
                dst_ref=part.at[me],
                send_sem=s_sem.at[d],
                recv_sem=r_sem.at[me],
                device_id=device(lax.rem(me + d, n)),
                device_id_type=MESH,
            )

        def copy_from(d):
            other = lax.rem(me + d, n)
            return pltpu.make_async_remote_copy(
                src_ref=part.at[other],
                dst_ref=part.at[other],
                send_sem=s_sem.at[d],
                recv_sem=r_sem.at[other],
                device_id=device(other),
                device_id_type=MESH,
            )

        def each(act):
            def body(d, _):
                act(d)
                return _

            lax.fori_loop(1, n, body, 0)

        return (
            lambda: each(lambda d: copy_to(d).start()),
            lambda: each(lambda d: copy_from(d).wait_recv()),
            lambda: each(lambda d: copy_to(d).wait_send()),
        )

    z_start, z_wait, z_sent = gather(part_z, ngz, gz, lambda o: (gy, o), zs_sem, zr_sem)
    y_start, y_wait, y_sent = gather(part_y, ngy, gy, lambda o: (o, gz), ys_sem, yr_sem)
    z_start()

    receive(2)
    take_rows(2, 0, cc)
    row_x, row_z = border_row(cc, 2, 0)
    hg[0, 0] = hg[0, 0] + row_on * row_x
    hg[2, 0] = hg[2, 0] + row_on * row_z
    col_x, col_y = border_col(2, 0)
    b_col[0] = b_col[0] + col_on * col_x
    b_col[1] = b_col[1] + col_on * col_y

    z_wait()
    part_y[gy] = jnp.sum(part_z[...], axis=0)
    y_start()

    def last_pass(r, _):
        curl = curl_forward(cc, 2, 0, r)
        out = [hg[c, r + 1] + curl[c] for c in range(3)]
        for c in range(3):
            hg[c, r + 1] = out[c]
        back = curl_backward(*out, hg[0, r], hg[2, r], b_col, r)
        for c in range(3):
            eg[c, r] = eg[c, r] - MAGNETIC_STEP * back[c]
        return _

    lax.fori_loop(0, rows, last_pass, 0)
    for copy in stores[4:]:
        copy.start()

    y_wait()
    whole = jnp.sum(part_y[...], axis=0)
    for label in range(count):
        tg_out[label] = jnp.sum(whole[label : label + 1, :]) * scale

    for k in range(3):
        finish(k)
    z_sent()
    y_sent()
    for copy in stores:
        copy.wait()


def solution(mesh):
    ngy, ngz = mesh.shape["gy"], mesh.shape["gz"]

    def on_device(*arrays):
        shape = arrays[0].shape
        _, rows, depth, width = shape
        count = arrays[12].shape[0]
        cells = rows * depth * width * ngy * ngz
        f32 = jnp.float32
        space = pl.BlockSpec(memory_space=pl.ANY)
        scalar = pl.BlockSpec(memory_space=pltpu.SMEM)
        three = jax.ShapeDtypeStruct(shape, f32)
        two = jax.ShapeDtypeStruct((2,) + shape[1:], f32)
        one = jax.ShapeDtypeStruct(shape[1:], f32)

        def vm(lead, wide=width):
            return pltpu.VMEM((lead, depth, wide), f32)

        def field(n, extra=0):
            return pltpu.VMEM((n, rows + extra, depth, width), f32)

        inputs = [
            pltpu.VMEM(arrays[i].shape, arrays[i].dtype) for i in (0, 1, 2, 3, 4, 5, 6, 7, 8, 9, 10, 11, 13)
        ]
        slots = -(-count // 8) * 8
        up, down, diag = sum(UP), sum(DOWN), sum(FIELDS)
        dma = pltpu.SemaphoreType.DMA
        scratch = inputs + [
            field(3, 1), field(3, 1), field(3, 1), field(3, 1),
            field(3), field(3), field(3), pltpu.VMEM(shape[1:], f32),
            field(3, 1), field(3, 1), field(3), field(3), field(3), field(2),
            pltpu.VMEM(shape[1:], f32),
            vm(2, LANES), vm(2, LANES),
            vm(up), vm(up), vm(down), vm(down),
            vm(up, LANES), vm(up, LANES), vm(down, LANES), vm(down, LANES),
            vm(diag, LANES), vm(diag, LANES),
            vm(count),
            pltpu.VMEM((ngz, slots, LANES), f32),
            pltpu.VMEM((ngy, slots, LANES), f32),
            dma((13,)), dma((6,)), dma((3, 6)), dma((3, 6)),
            dma((ngz,)), dma((ngz,)), dma((ngy,)), dma((ngy,)),
        ]
        moved = 4 * rows * depth * width * 40
        return pl.pallas_call(
            functools.partial(kernel, ngy, ngz, count, 1.0 / math.sqrt(cells)),
            out_shape=(three, three, three, three, two, one, jax.ShapeDtypeStruct((count,), f32)),
            in_specs=[scalar if i in (12, 14) else space for i in range(15)],
            out_specs=(space,) * 6 + (scalar,),
            scratch_shapes=scratch,
            cost_estimate=pl.CostEstimate(
                flops=500 * rows * depth * width, bytes_accessed=moved, transcendentals=0
            ),
            compiler_params=pltpu.CompilerParams(
                collective_id=0, has_side_effects=True, vmem_limit_bytes=56 * 1024 * 1024
            ),
        )(*arrays)

    field = P(None, "gy", None, "gz")
    cell = P("gy", None, "gz")
    return jax.shard_map(
        on_device,
        mesh=mesh,
        in_specs=(field,) * 10 + (cell, cell, P(), cell, P()),
        out_specs=(field,) * 5 + (cell, P()),
        check_vma=False,
    )
```

time: 154 us -> 50.5 us (0.33)
  waiting for transfers between devices: 43.3 us -> 0 us
  blocking collectives: 42.5 us -> 0 us
  Pallas kernels: 0 us -> 40.2 us
  starting transfers between devices: 30.1 us -> 0 us
  other arithmetic: 20.8 us -> 0 us
  local copies, waits for them, and re-layouts: 13.7 us -> 8.6 us
    ppermute x16 -> x0, waiting for transfers between devices: 43.3 us -> none  [shifted(): return lax.ppermute(block, axis, route)]
    psum x1 -> x0, blocking collectives: 42.5 us -> none  [on_device(): lax.psum(label_sums(material_labels, cell_grad, count), ('gy', 'gz'))]
    pallas_call x0 -> x1, Pallas kernels: none -> 40.2 us  [on_device(): pl.pallas_call(functools.partial(kernel, ngy, ngz, count, 1.0 / math.sqrt...]
    ppermute x16 -> x0, starting transfers between devices: 30.1 us -> none  [shifted(): return lax.ppermute(block, axis, route)]
    sub x23 -> x0, other arithmetic: 6.93 us -> none  [the longest x4 2.16 us: curl_forward(): along_z = jnp.concatenate([field[:, :, :, 1:], front_column], 3) - field]
    slice x35 -> x0, local copies, waits for them, and re-layouts: 4.87 us -> none  [the longest x4 1.84 us: curl_forward(): front_column = shifted(field[:, :, :, :1], 'gz', -1)]
    reduce_sum x6 -> x0, other arithmetic: 3.91 us -> none  [the longest x1 1.53 us: label_sums(): jnp.sum(jnp.where(material_labels == label, values, jnp.float32(0.0)))]
    add x3 -> x0, other arithmetic: 3.1 us -> none  [the longest x1 2.82 us: material_map(): inverse + jnp.where(material_labels == label, inverse_table[label], jnp.f...]
  transfers between devices with their start and end apart: 16 -> 0, of which waited for: 7 -> 0; matrix products, arithmetic and copies ran while one was open for 8% -> 0% of each run, Pallas kernels for 0% -> 0%
where the time goes in v1:
time: 50.5 us; the launch traced here: 50.1 us
  Pallas kernels  40.2 us (80%)
  local copies, waits for them, and re-layouts  8.6 us (17%)
  between operations  1.31 us (3%)
    pallas_call x1, Pallas kernels, on_device(): pl.pallas_call(functools.partial(kernel, ngy, ngz, count, 1.0 / math.sqrt...  40.2 us
    unnamed x19, local copies, waits for them, and re-layouts  8.6 us

profile of v1, /device:TPU:0, one launch (start us, length us, event | category | flops | bytes accessed | tf_op | source)
XLA Modules:
  0.0 50.1 jit_solution(1789677668072629392)
XLA Ops:
  1.3 40.2 %shard_map.198 = (f32[3,32,8,256]{3,2,1,0:T(8,128)}, f32[3,32,8,256]{3,2,1,0:T(8,128)}, f32[3,32,8,256]{3,2,1,0:T(8,128)}, f32[3,32,8,256]{3,2,1,0:T(8,128)}, f3...) custom-call(bf16[3,32,8,256]{3,2,1,0:T(8,128)(2,1)} %e_in.1, bf16[3,32,8,256]{3,2,1,0:T(8,128)(2,1)} %h_in.1, ...), custom_call_target="tpu_custom_call" | custom-call | flops 32768000 | bytes 10485760 | tf_op jit(solution)/shard_map/pallas_call | solution.py:579
  41.5 0.0 copy-start.2
  41.5 2.1 %copy.30 = f32[3,32,8,256]{3,2,1,0:T(8,128)} copy(f32[3,32,8,256]{3,2,1,0:T(8,128)} %get-tuple-element.14) | data formatting | bytes 1572864
  43.6 0.0 copy-done.2
  43.6 0.0 copy-start.1
  43.6 0.9 %copy.31 = f32[3,32,8,256]{3,2,1,0:T(8,128)} copy(f32[3,32,8,256]{3,2,1,0:T(8,128)S(1)} %copy-done.2) | data formatting | bytes 1572864
  44.5 0.5 %copy-done.1 = f32[3,32,8,256]{3,2,1,0:T(8,128)S(1)} copy-done((f32[3,32,8,256]{3,2,1,0:T(8,128)S(1)}, f32[3,32,8,256]{3,2,1,0:T(8,128)}, u32[]{:S(2)}) %copy-start.1) | copy-done | bytes 786456
  45.0 0.0 copy-start
  45.0 0.9 %copy.32 = f32[3,32,8,256]{3,2,1,0:T(8,128)} copy(f32[3,32,8,256]{3,2,1,0:T(8,128)S(1)} %copy-done.1) | data formatting | bytes 1572864
  45.9 0.5 %copy-done = f32[3,32,8,256]{3,2,1,0:T(8,128)S(1)} copy-done((f32[3,32,8,256]{3,2,1,0:T(8,128)S(1)}, f32[3,32,8,256]{3,2,1,0:T(8,128)}, u32[]{:S(2)}) %copy-start) | copy-done | bytes 786456
  46.5 0.0 copy-start.3
  46.5 0.9 %copy.33 = f32[3,32,8,256]{3,2,1,0:T(8,128)} copy(f32[3,32,8,256]{3,2,1,0:T(8,128)S(1)} %copy-done) | data formatting | bytes 1572864
  47.3 0.4 copy-done.3
  47.8 0.0 copy-start.4
  47.8 0.8 %copy.34 = f32[2,32,8,256]{3,2,1,0:T(8,128)} copy(f32[2,32,8,256]{3,2,1,0:T(8,128)S(1)} %copy-done.3) | data formatting | bytes 1048576
  48.6 0.3 copy-done.4
  48.9 0.0 copy-start.5
  48.9 0.7 %copy.35 = f32[32,8,256]{2,1,0:T(8,128)} copy(f32[32,8,256]{2,1,0:T(8,128)S(1)} %copy-done.4) | data formatting | bytes 524288
  49.6 0.0 copy-done.5
  49.6 0.5 %copy.36 = f32[4]{0:T(128)} copy(f32[4]{0:T(128)S(1)} %copy-done.5) | data formatting | bytes 32
Async XLA Ops:
  41.5 2.1 %copy-start.2 = (f32[3,32,8,256]{3,2,1,0:T(8,128)S(1)}, f32[3,32,8,256]{3,2,1,0:T(8,128)}, u32[]{:S(2)}) copy-start(f32[3,32,8,256]{3,2,1,0:T(8,128)} %get-tuple-element.15) | copy-start | bytes 2359300
  43.6 1.4 %copy-start.1 = (f32[3,32,8,256]{3,2,1,0:T(8,128)S(1)}, f32[3,32,8,256]{3,2,1,0:T(8,128)}, u32[]{:S(2)}) copy-start(f32[3,32,8,256]{3,2,1,0:T(8,128)} %get-tuple-element.16) | copy-start | bytes 2359300
  45.0 1.4 %copy-start = (f32[3,32,8,256]{3,2,1,0:T(8,128)S(1)}, f32[3,32,8,256]{3,2,1,0:T(8,128)}, u32[]{:S(2)}) copy-start(f32[3,32,8,256]{3,2,1,0:T(8,128)} %get-tuple-element.17) | copy-start | bytes 2359300
  46.5 1.3 %copy-start.3 = (f32[2,32,8,256]{3,2,1,0:T(8,128)S(1)}, f32[2,32,8,256]{3,2,1,0:T(8,128)}, u32[]{:S(2)}) copy-start(f32[2,32,8,256]{3,2,1,0:T(8,128)} %get-tuple-element.18) | copy-start | bytes 1572868
  47.8 1.1 %copy-start.4 = (f32[32,8,256]{2,1,0:T(8,128)S(1)}, f32[32,8,256]{2,1,0:T(8,128)}, u32[]{:S(2)}) copy-start(f32[32,8,256]{2,1,0:T(8,128)} %get-tuple-element.19) | copy-start | bytes 786436
  48.9 0.7 %copy-start.5 = (f32[4]{0:T(128)S(1)}, f32[4]{0:T(128)}, u32[]{:S(2)}) copy-start(f32[4]{0:T(128)} %get-tuple-element.20) | copy-start | bytes 52

commit v2 on v1

--- a/solution.py
+++ b/solution.py
@@ -22,6 +22,7 @@
 
 MESH = pl.DeviceIdType.MESH
 LANES = 128
+ROWS_PER_STEP = 4
 FIELDS = (1, 2, 1)
 BASES = (2, 2, 0)
 UP = tuple(3 * f + b for f, b in zip(FIELDS, BASES))
@@ -29,6 +30,78 @@
 UP_AT = tuple(sum(UP[:k]) for k in range(3))
 DOWN_AT = tuple(sum(DOWN[:k]) for k in range(3))
 DIAG_AT = tuple(sum(FIELDS[:k]) for k in range(3))
+
+
+class Shifts:
+    def __init__(self, depth, width):
+        self.depth, self.width, self.tiles = depth, width, width // LANES
+        self.lane = lax.broadcasted_iota(jnp.int32, (depth, LANES), 1)
+
+    def rows_of(self, v):
+        return [v[u : u + self.depth] for u in range(0, v.shape[0], self.depth)]
+
+    def widen(self, tile):
+        return tile if self.tiles == 1 else jnp.concatenate([tile] * self.tiles, axis=1)
+
+    def x_roll(self, v, shift, edge):
+        s = lax.broadcasted_iota(jnp.int32, (self.depth, v.shape[1]), 0)
+        rolled = [jnp.where(s == edge, 0.0, pltpu.roll(u, shift, 0)) for u in self.rows_of(v)]
+        return jnp.concatenate(rolled, axis=0)
+
+    def x_front(self, v):
+        return self.x_roll(v, self.depth - 1, self.depth - 1)
+
+    def x_behind(self, v):
+        return self.x_roll(v, 1, 0)
+
+    def z_front(self, v, tile, r):
+        lanes = self.lane
+        out = []
+        for u, row in enumerate(self.rows_of(v)):
+            border = pltpu.roll(tile, LANES - 1 - (r + u), 1)
+            rolled = pltpu.roll(row, self.width - 1, 1)
+            last = jnp.where(lanes == LANES - 1, border, rolled[:, self.width - LANES :])
+            if self.tiles > 1:
+                last = jnp.concatenate([rolled[:, : self.width - LANES], last], axis=1)
+            out.append(last)
+        return jnp.concatenate(out, axis=0)
+
+    def z_behind(self, v, tile, r):
+        lanes = self.lane
+        out = []
+        for u, row in enumerate(self.rows_of(v)):
+            border = pltpu.roll(tile, lax.rem(LANES - (r + u), LANES), 1)
+            rolled = pltpu.roll(row, 1, 1)
+            first = jnp.where(lanes == 0, border, rolled[:, :LANES])
+            if self.tiles > 1:
+                first = jnp.concatenate([first, rolled[:, LANES:]], axis=1)
+            out.append(first)
+        return jnp.concatenate(out, axis=0)
+
+    def curl_forward(self, ref, tile_x, tile_y, r, group):
+        def load(c, at):
+            return ref[c, pl.ds(at, group)].reshape(group * self.depth, self.width)
+
+        vx, vy, vz = load(0, r), load(1, r), load(2, r)
+        dy_x, dy_z = load(0, r + 1) - vx, load(2, r + 1) - vz
+        dz_x = self.z_front(vx, tile_x, r) - vx
+        dz_y = self.z_front(vy, tile_y, r) - vy
+        dx_y, dx_z = self.x_front(vy) - vy, self.x_front(vz) - vz
+        return (dy_z - dz_y, dz_x - dx_z, dx_y - dy_x)
+
+    def curl_backward(self, v, back_x, back_z, col, r):
+        vx, vy, vz = v
+
+        def behind(row, whole):
+            if whole.shape[0] == self.depth:
+                return row
+            return jnp.concatenate([row, whole[: -self.depth]], axis=0)
+
+        dy_x, dy_z = vx - behind(back_x, vx), vz - behind(back_z, vz)
+        dz_x = vx - self.z_behind(vx, col[0], r)
+        dz_y = vy - self.z_behind(vy, col[1], r)
+        dx_y, dx_z = vy - self.x_behind(vy), vz - self.x_behind(vz)
+        return (dy_z - dz_y, dz_x - dx_z, dx_y - dy_x)
 
 
 def kernel(
@@ -39,15 +112,15 @@
     e_in, h_in, p_in, q_in, n_in,
     es_in, hs_in, ps_in, qs_in, ns_in,
     lab_in, gain_in, table, src_in, start,
-    eg_out, hg_out, pg_out, qg_out, ng_out, cg_out, tg_out,
+    cc, hg, eg, pg, qg, ng, cg, tiles_out, b_col, tg_out,
     e_v, h_v, p_v, q_v, n_v,
     es_v, hs_v, ps_v, qs_v, ns_v,
     lab_v, gain_v, src_v,
-    ef, m, e1, ac, q1, q2, f1, k1, cc, hg, eg, pg, qg, ng, cg,
-    m_col, b_col,
+    ef, m, e1, ac, q1, q2, f1, k1,
+    m_col,
     yu_s, yu_r, yd_s, yd_r, zu_s, zu_r, zd_s, zd_r, a_r, b_r,
     sums, part_z, part_y,
-    in_sem, out_sem, send_sem, recv_sem,
+    in_sem, send_sem, recv_sem,
     zs_sem, zr_sem, ys_sem, yr_sem,
 ):
     gy = lax.axis_index("gy")
@@ -143,47 +216,30 @@
             def _(i=i, link=link):
                 remote(k, i, link).wait_send()
 
-    lane_wide = lax.broadcasted_iota(jnp.int32, (depth, width), 1)
-    sub_wide = lax.broadcasted_iota(jnp.int32, (depth, width), 0)
-    lane = lax.broadcasted_iota(jnp.int32, (depth, LANES), 1)
-    sub = lax.broadcasted_iota(jnp.int32, (depth, LANES), 0)
-    last_lane = lane_wide == width - 1
-    first_lane = lane_wide == 0
-    tiles = width // LANES
-
-    def widen(tile):
-        return tile if tiles == 1 else jnp.concatenate([tile] * tiles, axis=1)
-
-    def x_front(v):
-        s = sub_wide if v.shape[1] == width else sub
-        return jnp.where(s == depth - 1, 0.0, pltpu.roll(v, depth - 1, 0))
-
-    def x_behind(v):
-        return jnp.where(sub_wide == 0, 0.0, pltpu.roll(v, 1, 0))
-
-    def z_front(v, tile, r):
-        border = pltpu.roll(tile, LANES - 1 - r, 1)
-        return jnp.where(last_lane, widen(border), pltpu.roll(v, width - 1, 1))
-
-    def z_behind(v, tile, r):
-        border = pltpu.roll(tile, lax.rem(LANES - r, LANES), 1)
-        return jnp.where(first_lane, widen(border), pltpu.roll(v, 1, 1))
+    tools = Shifts(depth, width)
+    lane, tiles = tools.lane, tools.tiles
+    widen, x_front, z_front = tools.widen, tools.x_front, tools.z_front
+    group = math.gcd(rows, ROWS_PER_STEP)
 
     def curl_forward(ref, k, j, r):
-        f = FIELDS[k]
-        vx, vy, vz = ref[0, r], ref[1, r], ref[2, r]
-        dy_x, dy_z = ref[0, r + 1] - vx, ref[2, r + 1] - vz
-        dz_x = z_front(vx, zd_r[DOWN_AT[k] + j], r) - vx
-        dz_y = z_front(vy, zd_r[DOWN_AT[k] + f + j], r) - vy
-        dx_y, dx_z = x_front(vy) - vy, x_front(vz) - vz
-        return (dy_z - dz_y, dz_x - dx_z, dx_y - dy_x)
-
-    def curl_backward(vx, vy, vz, back_x, back_z, col, r):
-        dy_x, dy_z = vx - back_x, vz - back_z
-        dz_x = vx - z_behind(vx, col[0], r)
-        dz_y = vy - z_behind(vy, col[1], r)
-        dx_y, dx_z = vy - x_behind(vy), vz - x_behind(vz)
-        return (dy_z - dz_y, dz_x - dx_z, dx_y - dy_x)
+        at = DOWN_AT[k] + j
+        return tools.curl_forward(ref, zd_r[at], zd_r[at + FIELDS[k]], r, group)
+
+    def block(ref, c, r):
+        return ref[c, pl.ds(r, group)].astype(jnp.float32).reshape(group * depth, width)
+
+    def flat(ref, r):
+        return ref[pl.ds(r, group)].reshape(group * depth, width)
+
+    def put(ref, c, r, value):
+        ref[c, pl.ds(r, group)] = value.reshape(group, depth, width)
+
+    def over_rows(body):
+        def step(i, _):
+            body(i * group)
+            return _
+
+        lax.fori_loop(0, rows // group, step, 0)
 
     def border_row(ref, k, j):
         f = FIELDS[k]
@@ -205,7 +261,11 @@
     col_on = jnp.where(has_left, 1.0, 0.0).astype(jnp.float32)
 
     def pack(ref, slot, r, column):
-        ref[slot] = jnp.where(lane == r, jnp.broadcast_to(column, (depth, LANES)), ref[slot])
+        tile = ref[slot]
+        for u in range(column.shape[0] // depth):
+            part = jnp.broadcast_to(column[u * depth : (u + 1) * depth], (depth, LANES))
+            tile = jnp.where(lane == r + u, part, tile)
+        ref[slot] = tile
 
     def pack_first(k, j, r, vx, vy):
         f = FIELDS[k]
@@ -236,16 +296,15 @@
     loads[0].wait()
     loads[1].wait()
 
-    def first_pass(r, _):
-        v = [e_v[c, r].astype(jnp.float32) for c in range(3)]
-        for c in range(3):
-            ef[c, r] = v[c]
+    def first_pass(r):
+        v = [block(e_v, c, r) for c in range(3)]
+        for c in range(3):
+            put(ef, c, r, v[c])
         pack_first(0, 0, r, v[0], v[1])
         pack_last(0, 0, r, v)
-        pack_base(0, r, h_v[0, r].astype(jnp.float32), h_v[1, r].astype(jnp.float32))
-        return _
-
-    lax.fori_loop(0, rows, first_pass, 0)
+        pack_base(0, r, block(h_v, 0, r), block(h_v, 1, r))
+
+    over_rows(first_pass)
     stage_rows(0, 0, ef)
     yu_s[UP_AT[0] + 3] = h_v[0, rows - 1].astype(jnp.float32)
     yu_s[UP_AT[0] + 4] = h_v[2, rows - 1].astype(jnp.float32)
@@ -259,7 +318,9 @@
     begin = start[0].astype(jnp.float32)
     sine_first = jnp.sin(jnp.full((depth, LANES), SOURCE_OMEGA * begin, jnp.float32))
     sine_second = jnp.sin(jnp.full((depth, LANES), SOURCE_OMEGA * (begin + 1.0), jnp.float32))
-    sine_first, sine_second = widen(sine_first), widen(sine_second)
+    sine_first, sine_second = (
+        jnp.concatenate([widen(v)] * group, axis=0) for v in (sine_first, sine_second)
+    )
 
     for copy in loads[2:11]:
         copy.wait()
@@ -279,31 +340,31 @@
     m_col[0] = col_on * (zu_r[UP_AT[0] + 3] - MAGNETIC_STEP * col_x)
     m_col[1] = col_on * (zu_r[UP_AT[0] + 4] - MAGNETIC_STEP * col_y)
 
-    def forward_pass(r, _):
+    def forward_pass(r):
         curl = curl_forward(ef, 0, 0, r)
-        mid = [h_v[c, r].astype(jnp.float32) - MAGNETIC_STEP * curl[c] for c in range(3)]
-        for c in range(3):
-            m[c, r + 1] = mid[c]
-        c1 = curl_backward(*mid, m[0, r], m[2, r], m_col, r)
-        inverse = inverse_of(lab_v[r])
-        gain = gain_v[r].astype(jnp.float32)
-        source = src_v[r]
-        upper, lower = n_v[0, r].astype(jnp.float32), n_v[1, r].astype(jnp.float32)
+        mid = [block(h_v, c, r) - MAGNETIC_STEP * curl[c] for c in range(3)]
+        c1 = tools.curl_backward(mid, m[0, r], m[2, r], m_col, r)
+        for c in range(3):
+            put(m, c, r + 1, mid[c])
+        inverse = inverse_of(flat(lab_v, r))
+        gain = flat(gain_v, r).astype(jnp.float32)
+        source = flat(src_v, r)
+        upper, lower = block(n_v, 0, r), block(n_v, 1, r)
         gain_c, gain_s = COUPLING * gain, STIMULATED * gain
         couple = gain_c * (upper - lower)
         nexts, rates, polars = [], [], []
         work = None
         for c in range(3):
-            e, p, q = ef[c, r], p_v[c, r].astype(jnp.float32), q_v[c, r].astype(jnp.float32)
+            e, p, q = block(ef, c, r), block(p_v, c, r), block(q_v, c, r)
             rate = DAMPING * q - STIFFNESS * p + couple * e
             polars.append(p + TIME_STEP * rate)
             force = ELECTRIC_STEP * c1[c] - TIME_STEP * rate
             if c == 2:
                 force = force - sine_first * source
             new = e + inverse * force
-            q1[c, r] = rate
-            f1[c, r] = force
-            e1[c, r] = new
+            put(q1, c, r, rate)
+            put(f1, c, r, force)
+            put(e1, c, r, new)
             work = new * rate if work is None else work + new * rate
             nexts.append(new)
             rates.append(rate)
@@ -311,23 +372,22 @@
         upper_1 = upper + TIME_STEP * (PUMPING * (1.0 - upper - lower) - UPPER_DECAY * upper) - s
         lower_1 = lower + TIME_STEP * (UPPER_DECAY * upper - LOWER_DECAY * lower) + s
         couple_1 = gain_c * (upper_1 - lower_1)
-        k1[r] = couple_1
-        t2 = gain_s * (ns_v[1, r] - ns_v[0, r])
+        k1[pl.ds(r, group)] = couple_1.reshape(group, depth, width)
+        t2 = gain_s * (block(ns_v, 1, r) - block(ns_v, 0, r))
         half = ELECTRIC_STEP * inverse
         adj = []
         for c in range(3):
             rate = DAMPING * rates[c] - STIFFNESS * polars[c] + couple_1 * nexts[c]
-            q2[c, r] = rate
-            adj.append(half * (es_v[c, r] + t2 * rate))
-            ac[c, r] = adj[c]
+            put(q2, c, r, rate)
+            adj.append(half * (block(es_v, c, r) + t2 * rate))
+            put(ac, c, r, adj[c])
         pack_first(1, 0, r, nexts[0], nexts[1])
         pack_last(1, 0, r, nexts)
         pack_first(1, 1, r, adj[0], adj[1])
         pack_last(1, 1, r, adj)
-        pack_base(1, r, hs_v[0, r], hs_v[1, r])
-        return _
-
-    lax.fori_loop(0, rows, forward_pass, 0)
+        pack_base(1, r, block(hs_v, 0, r), block(hs_v, 1, r))
+
+    over_rows(forward_pass)
 
     stage_rows(1, 0, e1)
     stage_rows(1, 1, ac)
@@ -358,41 +418,40 @@
     drain_lower = -TIME_STEP * PUMPING
     keep_lower = 1.0 - TIME_STEP * LOWER_DECAY
 
-    def backward_pass(r, _):
+    def backward_pass(r):
         curl = curl_forward(e1, 1, 0, r)
-        last = [m[c, r + 1] - MAGNETIC_STEP * curl[c] for c in range(3)]
-        back_x, back_z = m[0, r], m[2, r]
-        m[0, r + 1] = last[0]
-        m[2, r + 1] = last[2]
-        c2 = curl_backward(*last, back_x, back_z, m_col, r)
+        last = [block(m, c, r + 1) - MAGNETIC_STEP * curl[c] for c in range(3)]
+        c2 = tools.curl_backward(last, m[0, r], m[2, r], m_col, r)
+        put(m, 0, r + 1, last[0])
+        put(m, 2, r + 1, last[2])
         curl = curl_forward(ac, 1, 1, r)
-        hb = [hs_v[c, r] + curl[c] for c in range(3)]
-        for c in range(3):
-            hg[c, r + 1] = hb[c]
-        eb = curl_backward(*hb, hg[0, r], hg[2, r], b_col, r)
-
-        labels = lab_v[r]
+        hb = [block(hs_v, c, r) + curl[c] for c in range(3)]
+        eb = tools.curl_backward(hb, hg[0, r], hg[2, r], b_col, r)
+        for c in range(3):
+            put(hg, c, r + 1, hb[c])
+
+        labels = flat(lab_v, r)
         inverse = inverse_of(labels)
-        gain = gain_v[r].astype(jnp.float32)
-        source = src_v[r]
+        gain = flat(gain_v, r).astype(jnp.float32)
+        source = flat(src_v, r)
         gain_c, gain_s = COUPLING * gain, STIMULATED * gain
-        seed_u, seed_l = ns_v[0, r], ns_v[1, r]
+        seed_u, seed_l = block(ns_v, 0, r), block(ns_v, 1, r)
         t2 = gain_s * (seed_l - seed_u)
-        couple_1 = k1[r]
+        couple_1 = flat(k1, r)
         total = None
         overlap = None
         b_e, a_p, a_q = [], [], []
         for c in range(3):
-            e, rate = e1[c, r], q2[c, r]
+            e, rate = block(e1, c, r), block(q2, c, r)
             force = ELECTRIC_STEP * c2[c] - TIME_STEP * rate
             if c == 2:
                 force = force - sine_second * source
             new = e + inverse * force
-            adj_e = es_v[c, r] + t2 * rate
+            adj_e = block(es_v, c, r) + t2 * rate
             term = adj_e * force
             total = term if total is None else total + term
-            seed_p = ps_v[c, r]
-            adj_q = qs_v[c, r] + t2 * new + TIME_STEP * (seed_p - inverse * adj_e)
+            seed_p = block(ps_v, c, r)
+            adj_q = block(qs_v, c, r) + t2 * new + TIME_STEP * (seed_p - inverse * adj_e)
             a_p.append(seed_p - STIFFNESS * adj_q)
             a_q.append(DAMPING * adj_q)
             b_e.append(adj_e + couple_1 * adj_q - MAGNETIC_STEP * eb[c])
@@ -402,50 +461,38 @@
         a_l = drain_lower * seed_u + keep_lower * seed_l - bend
 
         t1 = gain_s * (a_l - a_u)
-        upper, lower = n_v[0, r].astype(jnp.float32), n_v[1, r].astype(jnp.float32)
+        upper, lower = block(n_v, 0, r), block(n_v, 1, r)
         couple = gain_c * (upper - lower)
         overlap = None
         out = []
         for c in range(3):
-            rate = q1[c, r]
+            rate = block(q1, c, r)
             adj_e = b_e[c] + t1 * rate
-            total = total + adj_e * f1[c, r]
+            total = total + adj_e * block(f1, c, r)
             adj_f = inverse * adj_e
             curl_adj = ELECTRIC_STEP * adj_f
             out.append(curl_adj)
-            cc[c, r] = curl_adj
-            adj_q = a_q[c] + t1 * e1[c, r] + TIME_STEP * (a_p[c] - adj_f)
-            pg[c, r] = a_p[c] - STIFFNESS * adj_q
-            qg[c, r] = DAMPING * adj_q
-            eg[c, r] = adj_e + couple * adj_q
-            e = ef[c, r]
+            put(cc, c, r, curl_adj)
+            adj_q = a_q[c] + t1 * block(e1, c, r) + TIME_STEP * (a_p[c] - adj_f)
+            put(pg, c, r, a_p[c] - STIFFNESS * adj_q)
+            put(qg, c, r, DAMPING * adj_q)
+            put(eg, c, r, adj_e + couple * adj_q)
+            e = block(ef, c, r)
             overlap = adj_q * e if overlap is None else overlap + adj_q * e
         bend = gain_c * overlap
-        ng[0, r] = keep_upper * a_u + feed_upper * a_l + bend
-        ng[1, r] = drain_lower * a_u + keep_lower * a_l - bend
-        cg[r] = total
+        put(ng, 0, r, keep_upper * a_u + feed_upper * a_l + bend)
+        put(ng, 1, r, drain_lower * a_u + keep_lower * a_l - bend)
+        cg[pl.ds(r, group)] = total.reshape(group, depth, width)
         for label in range(count):
-            sums[label] = sums[label] + jnp.where(labels == label, total, 0.0)
+            mine = jnp.where(labels == label, total, 0.0)
+            sums[label] = sums[label] + sum(tools.rows_of(mine))
         pack_first(2, 0, r, out[0], out[1])
         pack_last(2, 0, r, out)
-        return _
-
-    lax.fori_loop(0, rows, backward_pass, 0)
+
+    over_rows(backward_pass)
 
     stage_rows(2, 0, cc)
     send(2)
-
-    stores = [
-        pltpu.make_async_copy(a, b, out_sem.at[i])
-        for i, (a, b) in enumerate(
-            (
-                (pg, pg_out), (qg, qg_out), (ng, ng_out), (cg, cg_out),
-                (hg.at[:, pl.ds(1, rows)], hg_out), (eg, eg_out),
-            )
-        )
-    ]
-    for copy in stores[:4]:
-        copy.start()
 
     mine = jnp.zeros(part_z.shape[1:], jnp.float32)
     part_sub = lax.broadcasted_iota(jnp.int32, mine.shape, 0)
@@ -505,20 +552,8 @@
     z_wait()
     part_y[gy] = jnp.sum(part_z[...], axis=0)
     y_start()
-
-    def last_pass(r, _):
-        curl = curl_forward(cc, 2, 0, r)
-        out = [hg[c, r + 1] + curl[c] for c in range(3)]
-        for c in range(3):
-            hg[c, r + 1] = out[c]
-        back = curl_backward(*out, hg[0, r], hg[2, r], b_col, r)
-        for c in range(3):
-            eg[c, r] = eg[c, r] - MAGNETIC_STEP * back[c]
-        return _
-
-    lax.fori_loop(0, rows, last_pass, 0)
-    for copy in stores[4:]:
-        copy.start()
+    tiles_out[0] = zd_r[DOWN_AT[2]]
+    tiles_out[1] = zd_r[DOWN_AT[2] + 1]
 
     y_wait()
     whole = jnp.sum(part_y[...], axis=0)
@@ -529,7 +564,49 @@
         finish(k)
     z_sent()
     y_sent()
-    for copy in stores:
+
+
+def last_kernel(
+    cc, hg, eg, pg, qg, ng, cg, tiles_in, b_col,
+    eg_out, hg_out, pg_out, qg_out, ng_out, cg_out,
+    hg_v, eg_v,
+    sem, row_sem,
+):
+    rows, depth, width = cg.shape
+    tools = Shifts(depth, width)
+    group = math.gcd(rows, ROWS_PER_STEP)
+    chunk = math.gcd(rows, 2 * group)
+    size = group * depth
+    ready = ((pg, pg_out), (qg, qg_out), (ng, ng_out), (cg, cg_out))
+    copies = [pltpu.make_async_copy(a, b, sem.at[i]) for i, (a, b) in enumerate(ready)]
+    for copy in copies:
+        copy.start()
+    hg_v[0, 0] = hg[0, 0]
+    hg_v[2, 0] = hg[2, 0]
+
+    def pass_rows(i, base):
+        r = base + i * group
+        curl = tools.curl_forward(cc, tiles_in[0], tiles_in[1], r, group)
+        out = [
+            hg[c, pl.ds(r + 1, group)].reshape(size, width) + curl[c] for c in range(3)
+        ]
+        back = tools.curl_backward(out, hg_v[0, r], hg_v[2, r], b_col, r)
+        for c in range(3):
+            hg_v[c, pl.ds(r + 1, group)] = out[c].reshape(group, depth, width)
+            value = eg[c, pl.ds(r, group)].reshape(size, width) - MAGNETIC_STEP * back[c]
+            eg_v[c, pl.ds(r, group)] = value.reshape(group, depth, width)
+        return base
+
+    for n, base in enumerate(range(0, rows, chunk)):
+        lax.fori_loop(0, chunk // group, pass_rows, base)
+        part = pl.ds(base, chunk)
+        for i, (a, b) in enumerate(
+            ((hg_v.at[:, pl.ds(base + 1, chunk)], hg_out.at[:, part]), (eg_v.at[:, part], eg_out.at[:, part]))
+        ):
+            copy = pltpu.make_async_copy(a, b, row_sem.at[n, i])
+            copy.start()
+            copies.append(copy)
+    for copy in copies:
         copy.wait()
 
 
@@ -563,32 +640,47 @@
         scratch = inputs + [
             field(3, 1), field(3, 1), field(3, 1), field(3, 1),
             field(3), field(3), field(3), pltpu.VMEM(shape[1:], f32),
-            field(3, 1), field(3, 1), field(3), field(3), field(3), field(2),
-            pltpu.VMEM(shape[1:], f32),
-            vm(2, LANES), vm(2, LANES),
+            vm(2, LANES),
             vm(up), vm(up), vm(down), vm(down),
             vm(up, LANES), vm(up, LANES), vm(down, LANES), vm(down, LANES),
             vm(diag, LANES), vm(diag, LANES),
             vm(count),
             pltpu.VMEM((ngz, slots, LANES), f32),
             pltpu.VMEM((ngy, slots, LANES), f32),
-            dma((13,)), dma((6,)), dma((3, 6)), dma((3, 6)),
+            dma((13,)), dma((3, 6)), dma((3, 6)),
             dma((ngz,)), dma((ngz,)), dma((ngy,)), dma((ngy,)),
         ]
         moved = 4 * rows * depth * width * 40
-        return pl.pallas_call(
+        kept = pl.BlockSpec(memory_space=pltpu.VMEM)
+        *values, table = pl.pallas_call(
             functools.partial(kernel, ngy, ngz, count, 1.0 / math.sqrt(cells)),
-            out_shape=(three, three, three, three, two, one, jax.ShapeDtypeStruct((count,), f32)),
+            out_shape=(
+                field(3, 1), field(3, 1), field(3), field(3), field(3), field(2),
+                pltpu.VMEM(shape[1:], f32), vm(2, LANES), vm(2, LANES),
+                jax.ShapeDtypeStruct((count,), f32),
+            ),
             in_specs=[scalar if i in (12, 14) else space for i in range(15)],
-            out_specs=(space,) * 6 + (scalar,),
+            out_specs=(kept,) * 9 + (scalar,),
             scratch_shapes=scratch,
             cost_estimate=pl.CostEstimate(
                 flops=500 * rows * depth * width, bytes_accessed=moved, transcendentals=0
             ),
             compiler_params=pltpu.CompilerParams(
-                collective_id=0, has_side_effects=True, vmem_limit_bytes=56 * 1024 * 1024
+                collective_id=0, has_side_effects=True, vmem_limit_bytes=58 * 1024 * 1024
             ),
         )(*arrays)
+        group = math.gcd(rows, ROWS_PER_STEP)
+        grads = pl.pallas_call(
+            last_kernel,
+            out_shape=(three, three, three, three, two, one),
+            in_specs=[kept] * 9,
+            out_specs=(space,) * 6,
+            scratch_shapes=[
+                field(3, 1), field(3), dma((4,)), dma((rows // math.gcd(rows, 2 * group), 2)),
+            ],
+            compiler_params=pltpu.CompilerParams(vmem_limit_bytes=24 * 1024 * 1024),
+        )(*values)
+        return (*grads, table)
 
     field = P(None, "gy", None, "gz")
     cell = P("gy", None, "gz")

time: 50.5 us -> 31.2 us (0.62)
  Pallas kernels: 40.2 us -> 28.6 us
  local copies, waits for them, and re-layouts: 8.6 us -> 1.17 us
    pallas_call x1, Pallas kernels: 40.2 us -> 26.2 us  [on_device(): pl.pallas_call(functools.partial(kernel, ngy, ngz, count, 1.0 / math.sqrt...]
    unnamed x19 -> x3, local copies, waits for them, and re-layouts: 8.6 us -> 1.17 us
    pallas_call x0 -> x1, Pallas kernels: none -> 2.33 us  [on_device(): pl.pallas_call(last_kernel, out_shape=(three, three, three, three, two, o...]
where the time goes in v2:
time: 31.2 us; the launch traced here: 31 us
  Pallas kernels  28.6 us (92%)
  between operations  1.31 us (4%)
  local copies, waits for them, and re-layouts  1.17 us (4%)
    pallas_call x1, Pallas kernels, on_device(): pl.pallas_call(functools.partial(kernel, ngy, ngz, count, 1.0 / math.sqrt...  26.2 us
    pallas_call x1, Pallas kernels, on_device(): pl.pallas_call(last_kernel, out_shape=(three, three, three, three, two, o...  2.33 us
    unnamed x3, local copies, waits for them, and re-layouts  1.17 us

profile of v2, /device:TPU:0, one launch (start us, length us, event | category | flops | bytes accessed | tf_op | source)
XLA Modules:
  0.0 31.0 jit_solution(11730463355100983142)
XLA Ops:
  1.3 26.2 %shard_map.198 = (f32[3,33,8,256]{3,2,1,0:T(8,128)S(1)}, f32[3,33,8,256]{3,2,1,0:T(8,128)S(1)}, f32[3,32,8,256]{3,2,1,0:T(8,128)S(1)}, f32[3,32,8,256]{3,2,1,0:T...) custom-call(bf16[3,32,8,256]{3,2,1,0:T(8,128)(2,1)} %e_in.1, ...), custom_call_target="tpu_custom_call" | custom-call | flops 32768000 | bytes 10485760 | tf_op jit(solution)/shard_map/pallas_call | solution.py:655
  27.5 2.3 %shard_map.199 = (f32[3,32,8,256]{3,2,1,0:T(8,128)}, f32[3,32,8,256]{3,2,1,0:T(8,128)}, f32[3,32,8,256]{3,2,1,0:T(8,128)}, f32[3,32,8,256]{3,2,1,0:T(8,128)}, f3...) custom-call(f32[3,33,8,256]{3,2,1,0:T(8,128)S(1)} %get-tuple-element.23.cc, f32[3,33,8,256]{3,2,1,0:T(8,128)S(1)} %get-tuple-element.24.hg, ...), custom_call_target="tpu_custom_call" | custom-call | tf_op jit(solution)/shard_map/pallas_call | solution.py:673
  29.9 0.0 copy-start
  29.9 0.7 %copy-done = f32[4]{0:T(128)S(1)} copy-done((f32[4]{0:T(128)S(1)}, f32[4]{0:T(128)}, u32[]{:S(2)}) %copy-start) | copy-done | bytes 40
  30.5 0.5 %copy.24 = f32[4]{0:T(128)} copy(f32[4]{0:T(128)S(1)} %copy-done) | data formatting | bytes 32
Async XLA Ops:
  29.9 0.7 %copy-start = (f32[4]{0:T(128)S(1)}, f32[4]{0:T(128)}, u32[]{:S(2)}) copy-start(f32[4]{0:T(128)} %get-tuple-element.52) | copy-start | bytes 52

commit v3 on v2

--- a/solution.py
+++ b/solution.py
@@ -108,20 +108,18 @@
     ngy,
     ngz,
     count,
-    scale,
     e_in, h_in, p_in, q_in, n_in,
     es_in, hs_in, ps_in, qs_in, ns_in,
     lab_in, gain_in, table, src_in, start,
-    cc, hg, eg, pg, qg, ng, cg, tiles_out, b_col, tg_out,
+    cc, hg, eg, pg, qg, ng, cg, tiles_out, b_col, whole_out,
     e_v, h_v, p_v, q_v, n_v,
     es_v, hs_v, ps_v, qs_v, ns_v,
     lab_v, gain_v, src_v,
     ef, m, e1, ac, q1, q2, f1, k1,
     m_col,
     yu_s, yu_r, yd_s, yd_r, zu_s, zu_r, zd_s, zd_r, a_r, b_r,
-    sums, part_z, part_y,
-    in_sem, send_sem, recv_sem,
-    zs_sem, zr_sem, ys_sem, yr_sem,
+    sums, part,
+    in_sem, send_sem, recv_sem, part_sem,
 ):
     gy = lax.axis_index("gy")
     gz = lax.axis_index("gz")
@@ -148,28 +146,18 @@
 
     barrier = pltpu.get_barrier_semaphore()
 
-    def greet_y(d, _):
-        pl.semaphore_signal(
-            barrier, inc=1, device_id=(lax.rem(gy + d, ngy), gz), device_id_type=MESH
-        )
+    devices = ngy * ngz
+    me = gy * ngz + gz
+
+    def peer(d):
+        other = lax.rem(me + d, devices)
+        return (lax.div(other, ngz), lax.rem(other, ngz))
+
+    def greet(d, _):
+        pl.semaphore_signal(barrier, inc=1, device_id=peer(d), device_id_type=MESH)
         return _
 
-    def greet_z(d, _):
-        pl.semaphore_signal(
-            barrier, inc=1, device_id=(gy, lax.rem(gz + d, ngz)), device_id_type=MESH
-        )
-        return _
-
-    lax.fori_loop(1, ngy, greet_y, 0)
-    lax.fori_loop(1, ngz, greet_z, 0)
-
-    @pl.when(diag_a)
-    def _():
-        pl.semaphore_signal(barrier, inc=1, device_id=(gy + 1, gz - 1), device_id_type=MESH)
-
-    @pl.when(diag_b)
-    def _():
-        pl.semaphore_signal(barrier, inc=1, device_id=(gy - 1, gz + 1), device_id_type=MESH)
+    lax.fori_loop(1, devices, greet, 0)
 
     def links(k):
         f = FIELDS[k]
@@ -309,10 +297,7 @@
     yu_s[UP_AT[0] + 3] = h_v[0, rows - 1].astype(jnp.float32)
     yu_s[UP_AT[0] + 4] = h_v[2, rows - 1].astype(jnp.float32)
 
-    greeted = (
-        (ngy - 1) + (ngz - 1) + jnp.where(diag_a, 1, 0) + jnp.where(diag_b, 1, 0)
-    )
-    pl.semaphore_wait(barrier, greeted)
+    pl.semaphore_wait(barrier, devices - 1)
     send(0)
 
     begin = start[0].astype(jnp.float32)
@@ -322,7 +307,18 @@
         jnp.concatenate([widen(v)] * group, axis=0) for v in (sine_first, sine_second)
     )
 
-    for copy in loads[2:11]:
+    for copy in loads[2:7]:
+        copy.wait()
+
+    def rate_pass(r):
+        gain = flat(gain_v, r).astype(jnp.float32)
+        couple = COUPLING * gain * (block(n_v, 0, r) - block(n_v, 1, r))
+        for c in range(3):
+            old = DAMPING * block(q_v, c, r) - STIFFNESS * block(p_v, c, r)
+            put(q1, c, r, old + couple * block(ef, c, r))
+
+    over_rows(rate_pass)
+    for copy in loads[7:11]:
         copy.wait()
 
     def inverse_of(labels):
@@ -351,18 +347,15 @@
         source = flat(src_v, r)
         upper, lower = block(n_v, 0, r), block(n_v, 1, r)
         gain_c, gain_s = COUPLING * gain, STIMULATED * gain
-        couple = gain_c * (upper - lower)
         nexts, rates, polars = [], [], []
         work = None
         for c in range(3):
-            e, p, q = block(ef, c, r), block(p_v, c, r), block(q_v, c, r)
-            rate = DAMPING * q - STIFFNESS * p + couple * e
-            polars.append(p + TIME_STEP * rate)
+            e, rate = block(ef, c, r), block(q1, c, r)
+            polars.append(block(p_v, c, r) + TIME_STEP * rate)
             force = ELECTRIC_STEP * c1[c] - TIME_STEP * rate
             if c == 2:
                 force = force - sine_first * source
             new = e + inverse * force
-            put(q1, c, r, rate)
             put(f1, c, r, force)
             put(e1, c, r, new)
             work = new * rate if work is None else work + new * rate
@@ -396,6 +389,26 @@
     send(1)
     for copy in loads[11:]:
         copy.wait()
+
+    def seed_pass(r):
+        inverse = inverse_of(flat(lab_v, r))
+        gain_s = STIMULATED * flat(gain_v, r).astype(jnp.float32)
+        t2 = gain_s * (block(ns_v, 1, r) - block(ns_v, 0, r))
+        total = None
+        for c in range(3):
+            rate = block(q2, c, r)
+            force = -TIME_STEP * rate
+            if c == 2:
+                force = force - sine_second * flat(src_v, r)
+            adj_e = block(es_v, c, r) + t2 * rate
+            total = adj_e * force if total is None else total + adj_e * force
+            new = block(e1, c, r) + inverse * force
+            bent = TIME_STEP * (block(ps_v, c, r) - inverse * adj_e)
+            put(qs_v, c, r, block(qs_v, c, r) + t2 * new + bent)
+            put(es_v, c, r, adj_e)
+        cg[pl.ds(r, group)] = total.reshape(group, depth, width)
+
+    over_rows(seed_pass)
     receive(1)
     take_rows(1, 0, e1)
     take_rows(1, 1, ac)
@@ -433,25 +446,20 @@
         labels = flat(lab_v, r)
         inverse = inverse_of(labels)
         gain = flat(gain_v, r).astype(jnp.float32)
-        source = flat(src_v, r)
         gain_c, gain_s = COUPLING * gain, STIMULATED * gain
         seed_u, seed_l = block(ns_v, 0, r), block(ns_v, 1, r)
         t2 = gain_s * (seed_l - seed_u)
         couple_1 = flat(k1, r)
-        total = None
+        total = flat(cg, r)
         overlap = None
+        curl_t = ELECTRIC_STEP * t2 * inverse
         b_e, a_p, a_q = [], [], []
         for c in range(3):
-            e, rate = block(e1, c, r), block(q2, c, r)
-            force = ELECTRIC_STEP * c2[c] - TIME_STEP * rate
-            if c == 2:
-                force = force - sine_second * source
-            new = e + inverse * force
-            adj_e = block(es_v, c, r) + t2 * rate
-            term = adj_e * force
-            total = term if total is None else total + term
+            e = block(e1, c, r)
+            adj_e = block(es_v, c, r)
+            total = total + ELECTRIC_STEP * adj_e * c2[c]
             seed_p = block(ps_v, c, r)
-            adj_q = block(qs_v, c, r) + t2 * new + TIME_STEP * (seed_p - inverse * adj_e)
+            adj_q = block(qs_v, c, r) + curl_t * c2[c]
             a_p.append(seed_p - STIFFNESS * adj_q)
             a_q.append(DAMPING * adj_q)
             b_e.append(adj_e + couple_1 * adj_q - MAGNETIC_STEP * eb[c])
@@ -494,51 +502,29 @@
     stage_rows(2, 0, cc)
     send(2)
 
-    mine = jnp.zeros(part_z.shape[1:], jnp.float32)
+    mine = jnp.zeros(part.shape[1:], jnp.float32)
     part_sub = lax.broadcasted_iota(jnp.int32, mine.shape, 0)
     for label in range(count):
         narrow = sum(sums[label, :, t * LANES : (t + 1) * LANES] for t in range(tiles))
         mine = jnp.where(part_sub == label, jnp.sum(narrow, axis=0, keepdims=True), mine)
-    part_z[gz] = mine
-
-    def gather(part, n, me, device, s_sem, r_sem):
-        def copy_to(d):
-            return pltpu.make_async_remote_copy(
-                src_ref=part.at[me],
-                dst_ref=part.at[me],
-                send_sem=s_sem.at[d],
-                recv_sem=r_sem.at[me],
-                device_id=device(lax.rem(me + d, n)),
-                device_id_type=MESH,
-            )
-
-        def copy_from(d):
-            other = lax.rem(me + d, n)
-            return pltpu.make_async_remote_copy(
-                src_ref=part.at[other],
-                dst_ref=part.at[other],
-                send_sem=s_sem.at[d],
-                recv_sem=r_sem.at[other],
-                device_id=device(other),
-                device_id_type=MESH,
-            )
-
-        def each(act):
-            def body(d, _):
-                act(d)
-                return _
-
-            lax.fori_loop(1, n, body, 0)
-
-        return (
-            lambda: each(lambda d: copy_to(d).start()),
-            lambda: each(lambda d: copy_from(d).wait_recv()),
-            lambda: each(lambda d: copy_to(d).wait_send()),
+    part[me] = mine
+
+    def part_copy(where, d):
+        return pltpu.make_async_remote_copy(
+            src_ref=part.at[where],
+            dst_ref=part.at[where],
+            send_sem=part_sem.at[0],
+            recv_sem=part_sem.at[1],
+            device_id=peer(d),
+            device_id_type=MESH,
         )
 
-    z_start, z_wait, z_sent = gather(part_z, ngz, gz, lambda o: (gy, o), zs_sem, zr_sem)
-    y_start, y_wait, y_sent = gather(part_y, ngy, gy, lambda o: (o, gz), ys_sem, yr_sem)
-    z_start()
+    def part_send(d, _):
+        part_copy(me, d).start()
+        return _
+
+    lax.fori_loop(1, devices, part_send, 0)
+    others = part_copy(pl.ds(0, devices - 1), 1)
 
     receive(2)
     take_rows(2, 0, cc)
@@ -549,26 +535,19 @@
     b_col[0] = b_col[0] + col_on * col_x
     b_col[1] = b_col[1] + col_on * col_y
 
-    z_wait()
-    part_y[gy] = jnp.sum(part_z[...], axis=0)
-    y_start()
     tiles_out[0] = zd_r[DOWN_AT[2]]
     tiles_out[1] = zd_r[DOWN_AT[2] + 1]
-
-    y_wait()
-    whole = jnp.sum(part_y[...], axis=0)
-    for label in range(count):
-        tg_out[label] = jnp.sum(whole[label : label + 1, :]) * scale
-
     for k in range(3):
         finish(k)
-    z_sent()
-    y_sent()
+    others.wait_recv()
+    whole_out[...] = jnp.sum(part[...], axis=0)
+    others.wait_send()
 
 
 def last_kernel(
-    cc, hg, eg, pg, qg, ng, cg, tiles_in, b_col,
-    eg_out, hg_out, pg_out, qg_out, ng_out, cg_out,
+    scale,
+    cc, hg, eg, pg, qg, ng, cg, tiles_in, b_col, whole,
+    eg_out, hg_out, pg_out, qg_out, ng_out, cg_out, tg_out,
     hg_v, eg_v,
     sem, row_sem,
 ):
@@ -581,6 +560,8 @@
     copies = [pltpu.make_async_copy(a, b, sem.at[i]) for i, (a, b) in enumerate(ready)]
     for copy in copies:
         copy.start()
+    for label in range(tg_out.shape[0]):
+        tg_out[label] = jnp.sum(whole[label : label + 1, :]) * scale
     hg_v[0, 0] = hg[0, 0]
     hg_v[2, 0] = hg[2, 0]
 
@@ -645,22 +626,20 @@
             vm(up, LANES), vm(up, LANES), vm(down, LANES), vm(down, LANES),
             vm(diag, LANES), vm(diag, LANES),
             vm(count),
-            pltpu.VMEM((ngz, slots, LANES), f32),
-            pltpu.VMEM((ngy, slots, LANES), f32),
-            dma((13,)), dma((3, 6)), dma((3, 6)),
-            dma((ngz,)), dma((ngz,)), dma((ngy,)), dma((ngy,)),
+            pltpu.VMEM((ngy * ngz, slots, LANES), f32),
+            dma((13,)), dma((3, 6)), dma((3, 6)), dma((2,)),
         ]
         moved = 4 * rows * depth * width * 40
         kept = pl.BlockSpec(memory_space=pltpu.VMEM)
-        *values, table = pl.pallas_call(
-            functools.partial(kernel, ngy, ngz, count, 1.0 / math.sqrt(cells)),
+        values = pl.pallas_call(
+            functools.partial(kernel, ngy, ngz, count),
             out_shape=(
                 field(3, 1), field(3, 1), field(3), field(3), field(3), field(2),
                 pltpu.VMEM(shape[1:], f32), vm(2, LANES), vm(2, LANES),
-                jax.ShapeDtypeStruct((count,), f32),
+                pltpu.VMEM((slots, LANES), f32),
             ),
             in_specs=[scalar if i in (12, 14) else space for i in range(15)],
-            out_specs=(kept,) * 9 + (scalar,),
+            out_specs=(kept,) * 10,
             scratch_shapes=scratch,
             cost_estimate=pl.CostEstimate(
                 flops=500 * rows * depth * width, bytes_accessed=moved, transcendentals=0
@@ -670,17 +649,17 @@
             ),
         )(*arrays)
         group = math.gcd(rows, ROWS_PER_STEP)
-        grads = pl.pallas_call(
-            last_kernel,
-            out_shape=(three, three, three, three, two, one),
-            in_specs=[kept] * 9,
-            out_specs=(space,) * 6,
+        table = jax.ShapeDtypeStruct((count,), f32)
+        return pl.pallas_call(
+            functools.partial(last_kernel, 1.0 / math.sqrt(cells)),
+            out_shape=(three, three, three, three, two, one, table),
+            in_specs=[kept] * 10,
+            out_specs=(space,) * 6 + (scalar,),
             scratch_shapes=[
                 field(3, 1), field(3), dma((4,)), dma((rows // math.gcd(rows, 2 * group), 2)),
             ],
             compiler_params=pltpu.CompilerParams(vmem_limit_bytes=24 * 1024 * 1024),
         )(*values)
-        return (*grads, table)
 
     field = P(None, "gy", None, "gz")
     cell = P("gy", None, "gz")

time: 31.2 us -> 30.2 us (0.968)
  local copies, waits for them, and re-layouts: 1.17 us -> 0 us
    unnamed x3 -> x0, local copies, waits for them, and re-layouts: 1.17 us -> none
where the time goes in v3:
time: 30.2 us; the launch traced here: 30.1 us
  Pallas kernels  28.8 us (95%)
  between operations  1.29 us (4%)
    pallas_call x1, Pallas kernels, on_device(): pl.pallas_call(functools.partial(kernel, ngy, ngz, count), out_shape=(fie...  25.8 us
    pallas_call x1, Pallas kernels, on_device(): pl.pallas_call(functools.partial(last_kernel, 1.0 / math.sqrt(cells)), ou...  2.96 us

profile of v3, /device:TPU:0, one launch (start us, length us, event | category | flops | bytes accessed | tf_op | source)
XLA Modules:
  0.0 30.1 jit_solution(17517088393734088663)
XLA Ops:
  1.3 25.8 %shard_map.198 = (f32[3,33,8,256]{3,2,1,0:T(8,128)S(1)}, f32[3,33,8,256]{3,2,1,0:T(8,128)S(1)}, f32[3,32,8,256]{3,2,1,0:T(8,128)S(1)}, f32[3,32,8,256]{3,2,1,0:T...) custom-call(bf16[3,32,8,256]{3,2,1,0:T(8,128)(2,1)} %e_in.1, ...), custom_call_target="tpu_custom_call" | custom-call | flops 32768000 | bytes 10485760 | tf_op jit(solution)/shard_map/pallas_call | solution.py:634
  27.1 3.0 %shard_map.199 = (f32[3,32,8,256]{3,2,1,0:T(8,128)}, f32[3,32,8,256]{3,2,1,0:T(8,128)}, f32[3,32,8,256]{3,2,1,0:T(8,128)}, f32[3,32,8,256]{3,2,1,0:T(8,128)}, f3...) custom-call(f32[3,33,8,256]{3,2,1,0:T(8,128)S(1)} %get-tuple-element.17.cc, ...), custom_call_target="tpu_custom_call" | custom-call | tf_op jit(solution)/shard_map/pallas_call | solution.py:653

commit v4 on v3

--- a/solution.py
+++ b/solution.py
@@ -133,7 +133,7 @@
     loads = [
         pltpu.make_async_copy(a, b, in_sem.at[i]) for i, (a, b) in enumerate(pairs)
     ]
-    for copy in loads:
+    for copy in loads[:2]:
         copy.start()
 
     for ref in (yu_r, yd_r, zu_r, zd_r, a_r, b_r, zu_s, zd_s):
@@ -283,6 +283,8 @@
 
     loads[0].wait()
     loads[1].wait()
+    for copy in loads[2:]:
+        copy.start()
 
     def first_pass(r):
         v = [block(e_v, c, r) for c in range(3)]
@@ -560,8 +562,6 @@
     copies = [pltpu.make_async_copy(a, b, sem.at[i]) for i, (a, b) in enumerate(ready)]
     for copy in copies:
         copy.start()
-    for label in range(tg_out.shape[0]):
-        tg_out[label] = jnp.sum(whole[label : label + 1, :]) * scale
     hg_v[0, 0] = hg[0, 0]
     hg_v[2, 0] = hg[2, 0]
 
@@ -587,6 +587,8 @@
             copy = pltpu.make_async_copy(a, b, row_sem.at[n, i])
             copy.start()
             copies.append(copy)
+    for label in range(tg_out.shape[0]):
+        tg_out[label] = jnp.sum(whole[label : label + 1, :]) * scale
     for copy in copies:
         copy.wait()
 

time: 30.2 us -> 30.1 us (level)
  no operation moved by 1% of the time
where the time goes in v4:
time: 30.1 us; the launch traced here: 29.9 us
  Pallas kernels  28.6 us (95%)
  between operations  1.29 us (4%)
    pallas_call x1, Pallas kernels, on_device(): pl.pallas_call(functools.partial(kernel, ngy, ngz, count), out_shape=(fie...  25.8 us
    pallas_call x1, Pallas kernels, on_device(): pl.pallas_call(functools.partial(last_kernel, 1.0 / math.sqrt(cells)), ou...  2.8 us

profile of v4, /device:TPU:0, one launch (start us, length us, event | category | flops | bytes accessed | tf_op | source)
XLA Modules:
  0.0 29.9 jit_solution(9628998210459410551)
XLA Ops:
  1.3 25.8 %shard_map.198 = (f32[3,33,8,256]{3,2,1,0:T(8,128)S(1)}, f32[3,33,8,256]{3,2,1,0:T(8,128)S(1)}, f32[3,32,8,256]{3,2,1,0:T(8,128)S(1)}, f32[3,32,8,256]{3,2,1,0:T...) custom-call(bf16[3,32,8,256]{3,2,1,0:T(8,128)(2,1)} %e_in.1, ...), custom_call_target="tpu_custom_call" | custom-call | flops 32768000 | bytes 10485760 | tf_op jit(solution)/shard_map/pallas_call | solution.py:636
  27.1 2.8 %shard_map.199 = (f32[3,32,8,256]{3,2,1,0:T(8,128)}, f32[3,32,8,256]{3,2,1,0:T(8,128)}, f32[3,32,8,256]{3,2,1,0:T(8,128)}, f32[3,32,8,256]{3,2,1,0:T(8,128)}, f3...) custom-call(f32[3,33,8,256]{3,2,1,0:T(8,128)S(1)} %get-tuple-element.17.cc, ...), custom_call_target="tpu_custom_call" | custom-call | tf_op jit(solution)/shard_map/pallas_call | solution.py:655
